TPU v7x, 256 devices: a whole 4x4x8 slice. The times are simulated.
256 devices in a mesh: chan: 32 (over z, x_hi, core), tm: 8 (over x_lo, y).
Axes of the slice: x: 4 (x_hi: 2, x_lo: 2; x = x_hi * 2 + x_lo), y: 4, z: 8, core: 2. Of those that a mesh axis runs over, the one named last changes fastest.
Arguments:
- record: float32 [4096, 8192], P('chan', 'tm'), may hold values from -6 to 6
- alive: int32 [4096], P('chan'), may hold values 0 or 1
- taps: float32 [64], replicated, may hold values from -0.75 to 0.75
- pattern: int32 [256, 2], P(('chan', 'tm')), may hold values from 0 to 3
Outputs:
- correlations: float32 [256, 2, 16, 16, 1024], P(('chan', 'tm'))
Inputs may be any that keep to these rules, and one draw needn't show every extreme that they name: `pattern`: partner blocks that lie past the last channel count as zeros.
All inputs are finite; a program needn't handle non-finite values. No bound on the sum of `alive` on one device may be relied on, other than what follows from the above.
Results may differ from a plain program's by a relative error of at most 0.0037.
Values may be sent and summed in bfloat16 or wider, within the bound.
A program may use at most 128 MiB of HBM per device.

v0:
```python
import math

import jax
import jax.numpy as jnp
from jax import lax
from jax.sharding import PartitionSpec as P

TAPS = 64
HALF_WIN = 256
LAG = 512
BLOCK = 16
PAIR_SPAN = 4
PAIRS = 2


def extended_2(value, sides, width):
    for axis, dim in sides:
        devices, length = (lax.axis_size(axis), value.shape[dim])
        up = [(i, (i + 1) % devices) for i in range(devices - 1)]
        down = [(j, i) for i, j in up]
        last = lax.slice_in_dim(value, length - width, length, axis=dim)
        leading = lax.slice_in_dim(value, 0, width, axis=dim)
        before = lax.ppermute(last, axis, up)
        after = lax.ppermute(leading, axis, down)
        value = jnp.concatenate([before, value, after], axis=dim)
    return value


def from_behind(block, axis, distance):
    devices = range(lax.axis_size(axis))
    route = [(i - distance, i) for i in devices if i - distance in devices]
    return lax.ppermute(block, axis, route)


def band_matrix(taps, row_count):
    length = row_count + taps.shape[0]
    widened = jnp.concatenate([taps, jnp.zeros((row_count + 1,), taps.dtype)])
    repeated = jnp.broadcast_to(widened[None, :], (row_count, length + 1))
    return repeated.reshape(-1)[: row_count * length].reshape(row_count, length)


def running_level(magnitude):
    count, times = magnitude.shape
    width = 2 * HALF_WIN
    padded = jnp.pad(magnitude, ((0, 0), (HALF_WIN, HALF_WIN)))
    tiles = padded.reshape(count, times // width + 1, width)
    windows = jnp.concatenate([tiles[:, :-1], tiles[:, 1:]], -1)
    inner = jnp.arange(2 * width)[:, None]
    outer = jnp.arange(width)[None, :]
    boxcar = ((inner >= outer) & (inner <= outer + width)).astype(jnp.float32)
    summed = jnp.einsum(
        "cnx,xt->cnt",
        windows,
        boxcar,
        precision=lax.Precision.HIGHEST,
        preferred_element_type=jnp.float32,
    )
    return summed.reshape(count, times) / (width + 1)


def normalize(filtered):
    level = running_level(jnp.abs(filtered))
    return (filtered / (level + 1e-05)).astype(jnp.bfloat16)


def toeplitz_tiles(windows, tile_len):
    leading = windows.shape[:-1]
    widened = jnp.concatenate([windows, jnp.zeros(leading + (1,), windows.dtype)], -1)
    repeated = jnp.broadcast_to(widened[..., None, :], leading + (tile_len, 2 * tile_len + 1))
    flat = repeated.reshape(leading + (tile_len * (2 * tile_len + 1),))[
        ..., : tile_len * 2 * tile_len
    ]
    return flat.reshape(leading + (tile_len, 2 * tile_len))[..., tile_len:]


def correlate(mine, partners):
    block_count, width, times = mine.shape
    tile_len = LAG // 4
    quarters = 2 * LAG // tile_len
    tile_count = times // tile_len
    kept = tile_count + 1
    group = max(1, -(-kept // 8))
    turns = -(-kept // group)
    padded_count = turns * group
    mine_tiles = jnp.pad(mine, ((0, 0), (0, 0), (tile_len, (padded_count - tile_count) * tile_len)))
    mine_tiles = mine_tiles.reshape(block_count, width, padded_count + 1, tile_len)
    their_count = padded_count + quarters - 1
    their_tiles = jnp.pad(
        partners, ((0, 0), (0, 0), (0, 0), (LAG, their_count * tile_len - times - LAG))
    )
    their_tiles = their_tiles.reshape(block_count, PAIRS, BLOCK, their_count, tile_len)

    def advance(turn, total):
        first = turn * group
        nearby = lax.dynamic_slice_in_dim(mine_tiles, first, group + 1, 2)
        windows = jnp.concatenate([nearby[:, :, :-1], nearby[:, :, 1:]], -1)
        toeplitz = toeplitz_tiles(windows, tile_len)
        span = lax.dynamic_slice_in_dim(their_tiles, first, group + quarters - 1, 3)
        parts = [
            jnp.einsum(
                "bpjkw,bikuw->bpiju",
                span[:, :, :, quarter : quarter + group],
                toeplitz,
                preferred_element_type=jnp.float32,
            )
            for quarter in range(quarters)
        ]
        return total + jnp.stack(parts, 4)

    start = jnp.zeros((block_count, PAIRS, width, BLOCK, quarters, tile_len), jnp.float32)
    summed = lax.fori_loop(0, turns, advance, start)
    return summed.reshape(block_count, PAIRS, width, BLOCK, 2 * LAG)


def body(record, alive, taps, pattern):
    row_count, time_span = record.shape
    tm_count = lax.axis_size("tm")
    mine_count = row_count // tm_count
    reach_rows = (PAIR_SPAN - 1) * BLOCK
    lively = alive.astype(jnp.float32)[:, None]
    masked = record * lively
    rimmed = extended_2(masked, (("chan", 0),), TAPS // 2)
    filtered = lively * jnp.dot(
        band_matrix(taps, row_count),
        rimmed,
        precision=lax.Precision.HIGHEST,
        preferred_element_type=jnp.float32,
    )
    whole = lax.all_to_all(filtered, "tm", split_axis=0, concat_axis=1, tiled=True)
    normed = normalize(whole)
    needed = -(-reach_rows // mine_count)
    pieces = [normed]
    for step in range(1, needed + 1):
        pieces.append(from_behind(normed, ("chan", "tm"), -step))
    extended = jnp.concatenate(pieces, 0)
    times = extended.shape[1]
    block_count = mine_count // BLOCK
    starts = (jnp.arange(block_count, dtype=jnp.int32)[:, None] + pattern) * BLOCK

    def take_block(first):
        return lax.dynamic_slice_in_dim(extended, first, BLOCK, 0)

    partners = jax.vmap(jax.vmap(take_block))(starts)
    mine = extended[:mine_count].reshape(block_count, BLOCK, times)
    return correlate(mine, partners) * (1.0 / math.sqrt(times))


def solution(mesh):
    placed = (P("chan", "tm"), P("chan"), P(), P(("chan", "tm"), None))
    return jax.shard_map(
        body,
        mesh=mesh,
        in_specs=placed,
        out_specs=P(("chan", "tm"), None, None, None, None),
        check_vma=False,
    )
```

profile of v0, /device:TPU:168, one launch (start us, length us, event | category | flops | bytes accessed | tf_op | source)
XLA Modules:
  0.0 636.6 jit_solution(12159033162347894210)
XLA Ops:
  19.7 9.1 %all-to-all-done = f32[8,16,1024]{2,1,0:T(8,128)S(1)} async-done(((f32[8,16,1024]{2,1,0:T(8,128)}), f32[8,16,1024]{2,1,0:T(8,128)S(1)}, u32[]{:S(2)}, u32[]{:S(2)}) %all-to-all-start) | async-done | bytes 524320 | tf_op jit(solution)/shard_map/all_to_all | solution.py:129
  51.6 9.9 %collective-permute-done.4 = bf16[16,8192]{1,0:T(8,128)(2,1)} collective-permute-done((bf16[16,8192]{1,0:T(8,128)(2,1)S(1)}, bf16[16,8192]{1,0:T(8,128)(2,1)}, u32[]{:S(2)}, u32[]{:S(2)}) %collective-permute-start.4) | collective-permute-done | bytes 262176 | tf_op jit(solution)/shard_map/ppermute | solution.py:32
  65.9 567.8 %while.16 = (s32[]{:T(128)}, f32[1,2,16,16,8,128]{5,3,1,2,4,0:T(8,128)S(1)}, bf16[1,16,73,128]{3,1,2,0:T(8,128)(2,1)}, bf16[1,2,16,79,128]{4,3,2,1,0:T(8,128)(2,...) while((s32[]{:T(128)}, ...), condition=%wide.region_1.2_spmd.clone, body=%wide.region_0.1_spmd.clone.sunk | while | flops 1209230208 | bytes 152598512 | solution.py:111
  66.9 6.3 broadcast_in_dim.42
  73.2 22.5 %broadcast_in_dim.43 = bf16[1,16,9,32896]{3,1,2,0:T(8,128)(2,1)} reshape(bf16[16,9,128,257]{3,2,0,1:T(8,128)(2,1)} %broadcast_in_dim.42) | data formatting | bytes 18948096 | tf_op jit(solution)/shard_map/while/body/eval_jaxpr/broadcast_in_dim | solution.py:69
  95.7 8.1 %slice.179 = bf16[1,16,9,32768]{3,1,2,0:T(8,128)(2,1)} slice(bf16[1,16,9,32896]{3,1,2,0:T(8,128)(2,1)} %broadcast_in_dim.43), slice={[0:1], [0:16], [0:9], [0:32768]} | slice | bytes 18874368 | tf_op jit(solution)/shard_map/while/body/eval_jaxpr/slice | solution.py:70
  103.9 10.2 %copy.110 = bf16[18,8,128,256]{3,2,1,0:T(8,128)(2,1)} copy(bf16[18,8,128,256]{3,1,2,0:T(8,128)(2,1)} %bitcast.233) | data formatting | bytes 18874368 | tf_op jit(solution)/shard_map/while
  137.9 6.3 broadcast_in_dim.42
  144.2 22.5 %broadcast_in_dim.43 = bf16[1,16,9,32896]{3,1,2,0:T(8,128)(2,1)} reshape(bf16[16,9,128,257]{3,2,0,1:T(8,128)(2,1)} %broadcast_in_dim.42) | data formatting | bytes 18948096 | tf_op jit(solution)/shard_map/while/body/eval_jaxpr/broadcast_in_dim | solution.py:69
  166.7 8.1 %slice.179 = bf16[1,16,9,32768]{3,1,2,0:T(8,128)(2,1)} slice(bf16[1,16,9,32896]{3,1,2,0:T(8,128)(2,1)} %broadcast_in_dim.43), slice={[0:1], [0:16], [0:9], [0:32768]} | slice | bytes 18874368 | tf_op jit(solution)/shard_map/while/body/eval_jaxpr/slice | solution.py:70
  174.8 10.2 %copy.110 = bf16[18,8,128,256]{3,2,1,0:T(8,128)(2,1)} copy(bf16[18,8,128,256]{3,1,2,0:T(8,128)(2,1)} %bitcast.233) | data formatting | bytes 18874368 | tf_op jit(solution)/shard_map/while
  208.8 6.3 broadcast_in_dim.42
  215.1 22.5 %broadcast_in_dim.43 = bf16[1,16,9,32896]{3,1,2,0:T(8,128)(2,1)} reshape(bf16[16,9,128,257]{3,2,0,1:T(8,128)(2,1)} %broadcast_in_dim.42) | data formatting | bytes 18948096 | tf_op jit(solution)/shard_map/while/body/eval_jaxpr/broadcast_in_dim | solution.py:69
  237.6 8.1 %slice.179 = bf16[1,16,9,32768]{3,1,2,0:T(8,128)(2,1)} slice(bf16[1,16,9,32896]{3,1,2,0:T(8,128)(2,1)} %broadcast_in_dim.43), slice={[0:1], [0:16], [0:9], [0:32768]} | slice | bytes 18874368 | tf_op jit(solution)/shard_map/while/body/eval_jaxpr/slice | solution.py:70
  245.8 10.2 %copy.110 = bf16[18,8,128,256]{3,2,1,0:T(8,128)(2,1)} copy(bf16[18,8,128,256]{3,1,2,0:T(8,128)(2,1)} %bitcast.233) | data formatting | bytes 18874368 | tf_op jit(solution)/shard_map/while
  286.1 22.5 %broadcast_in_dim.43 = bf16[1,16,9,32896]{3,1,2,0:T(8,128)(2,1)} reshape(bf16[16,9,128,257]{3,2,0,1:T(8,128)(2,1)} %broadcast_in_dim.42) | data formatting | bytes 18948096 | tf_op jit(solution)/shard_map/while/body/eval_jaxpr/broadcast_in_dim | solution.py:69
  308.6 8.1 %slice.179 = bf16[1,16,9,32768]{3,1,2,0:T(8,128)(2,1)} slice(bf16[1,16,9,32896]{3,1,2,0:T(8,128)(2,1)} %broadcast_in_dim.43), slice={[0:1], [0:16], [0:9], [0:32768]} | slice | bytes 18874368 | tf_op jit(solution)/shard_map/while/body/eval_jaxpr/slice | solution.py:70
  316.7 10.2 %copy.110 = bf16[18,8,128,256]{3,2,1,0:T(8,128)(2,1)} copy(bf16[18,8,128,256]{3,1,2,0:T(8,128)(2,1)} %bitcast.233) | data formatting | bytes 18874368 | tf_op jit(solution)/shard_map/while
  350.8 6.3 broadcast_in_dim.42
  357.0 22.5 %broadcast_in_dim.43 = bf16[1,16,9,32896]{3,1,2,0:T(8,128)(2,1)} reshape(bf16[16,9,128,257]{3,2,0,1:T(8,128)(2,1)} %broadcast_in_dim.42) | data formatting | bytes 18948096 | tf_op jit(solution)/shard_map/while/body/eval_jaxpr/broadcast_in_dim | solution.py:69
  379.5 8.1 %slice.179 = bf16[1,16,9,32768]{3,1,2,0:T(8,128)(2,1)} slice(bf16[1,16,9,32896]{3,1,2,0:T(8,128)(2,1)} %broadcast_in_dim.43), slice={[0:1], [0:16], [0:9], [0:32768]} | slice | bytes 18874368 | tf_op jit(solution)/shard_map/while/body/eval_jaxpr/slice | solution.py:70
  387.7 10.2 %copy.110 = bf16[18,8,128,256]{3,2,1,0:T(8,128)(2,1)} copy(bf16[18,8,128,256]{3,1,2,0:T(8,128)(2,1)} %bitcast.233) | data formatting | bytes 18874368 | tf_op jit(solution)/shard_map/while
  428.0 22.5 %broadcast_in_dim.43 = bf16[1,16,9,32896]{3,1,2,0:T(8,128)(2,1)} reshape(bf16[16,9,128,257]{3,2,0,1:T(8,128)(2,1)} %broadcast_in_dim.42) | data formatting | bytes 18948096 | tf_op jit(solution)/shard_map/while/body/eval_jaxpr/broadcast_in_dim | solution.py:69
  450.5 8.1 %slice.179 = bf16[1,16,9,32768]{3,1,2,0:T(8,128)(2,1)} slice(bf16[1,16,9,32896]{3,1,2,0:T(8,128)(2,1)} %broadcast_in_dim.43), slice={[0:1], [0:16], [0:9], [0:32768]} | slice | bytes 18874368 | tf_op jit(solution)/shard_map/while/body/eval_jaxpr/slice | solution.py:70
  458.6 10.2 %copy.110 = bf16[18,8,128,256]{3,2,1,0:T(8,128)(2,1)} copy(bf16[18,8,128,256]{3,1,2,0:T(8,128)(2,1)} %bitcast.233) | data formatting | bytes 18874368 | tf_op jit(solution)/shard_map/while
  492.7 6.3 broadcast_in_dim.42
  498.9 22.5 %broadcast_in_dim.43 = bf16[1,16,9,32896]{3,1,2,0:T(8,128)(2,1)} reshape(bf16[16,9,128,257]{3,2,0,1:T(8,128)(2,1)} %broadcast_in_dim.42) | data formatting | bytes 18948096 | tf_op jit(solution)/shard_map/while/body/eval_jaxpr/broadcast_in_dim | solution.py:69
  521.4 8.1 %slice.179 = bf16[1,16,9,32768]{3,1,2,0:T(8,128)(2,1)} slice(bf16[1,16,9,32896]{3,1,2,0:T(8,128)(2,1)} %broadcast_in_dim.43), slice={[0:1], [0:16], [0:9], [0:32768]} | slice | bytes 18874368 | tf_op jit(solution)/shard_map/while/body/eval_jaxpr/slice | solution.py:70
  529.6 10.2 %copy.110 = bf16[18,8,128,256]{3,2,1,0:T(8,128)(2,1)} copy(bf16[18,8,128,256]{3,1,2,0:T(8,128)(2,1)} %bitcast.233) | data formatting | bytes 18874368 | tf_op jit(solution)/shard_map/while
  569.9 22.5 %broadcast_in_dim.43 = bf16[1,16,9,32896]{3,1,2,0:T(8,128)(2,1)} reshape(bf16[16,9,128,257]{3,2,0,1:T(8,128)(2,1)} %broadcast_in_dim.42) | data formatting | bytes 18948096 | tf_op jit(solution)/shard_map/while/body/eval_jaxpr/broadcast_in_dim | solution.py:69
  592.4 8.1 %slice.179 = bf16[1,16,9,32768]{3,1,2,0:T(8,128)(2,1)} slice(bf16[1,16,9,32896]{3,1,2,0:T(8,128)(2,1)} %broadcast_in_dim.43), slice={[0:1], [0:16], [0:9], [0:32768]} | slice | bytes 18874368 | tf_op jit(solution)/shard_map/while/body/eval_jaxpr/slice | solution.py:70
  600.5 10.2 %copy.110 = bf16[18,8,128,256]{3,2,1,0:T(8,128)(2,1)} copy(bf16[18,8,128,256]{3,1,2,0:T(8,128)(2,1)} %bitcast.233) | data formatting | bytes 18874368 | tf_op jit(solution)/shard_map/while
  (176 shorter events, 260.4 us)
Async XLA Ops:
  0.0 19.6 %copy-start.2 = (s32[1,2]{1,0:T(1,128)S(1)}, s32[1,2]{1,0:T(1,128)}, u32[]{:S(2)}) copy-start(s32[1,2]{1,0:T(1,128)} %param.9) | copy-start | bytes 28
  1.8 9.1 %collective-permute-start = (f32[32,1024]{1,0:T(8,128)S(1)}, f32[32,1024]{1,0:T(8,128)S(1)}, u32[]{:S(2)}, u32[]{:S(2)}) collective-permute-start(f32[32,1024]{1,0:T(8,128)S(1)} %get-tuple-element.148), channel_id=1, source_target_pairs={{0,8},{8,16},{16,24},{24,32},{32,40},{40,48},{48,56},{56,64},{64,7... | collective-permute-start | bytes 393224 | tf_op jit(solution)/shard_map/ppermute | solution.py:23
  3.8 8.6 %collective-permute-start.1 = (f32[32,1024]{1,0:T(8,128)S(1)}, f32[32,1024]{1,0:T(8,128)S(1)}, u32[]{:S(2)}, u32[]{:S(2)}) collective-permute-start(f32[32,1024]{1,0:T(8,128)S(1)} %get-tuple-element.149), channel_id=1, source_target_pairs={{8,0},{16,8},{24,16},{32,24},{40,32},{48,40},{56,48},{64,56},{72,6... | collective-permute-start | bytes 393224 | tf_op jit(solution)/shard_map/ppermute | solution.py:24
  13.8 15.1 %all-to-all-start = ((f32[8,16,1024]{2,1,0:T(8,128)}), f32[8,16,1024]{2,1,0:T(8,128)S(1)}, u32[]{:S(2)}, u32[]{:S(2)}) async-start(f32[8,16,1024]{2,1,0:T(8,128)} %bitcast), calls=%async_computation | async-start | bytes 1048576 | tf_op jit(solution)/shard_map/all_to_all | solution.py:129
  34.5 0.8 copy-start.1
  35.3 14.9 %collective-permute-start.2 = (bf16[16,8192]{1,0:T(8,128)(2,1)S(1)}, bf16[16,8192]{1,0:T(8,128)(2,1)}, u32[]{:S(2)}, u32[]{:S(2)}) collective-permute-start(bf16[16,8192]{1,0:T(8,128)(2,1)S(1)} %divide_convert_fusion), channel_id=1, source_target_pairs={{1,0},{2,1},{3,2},{4,3},{5,4},{6,5},{7,6},{8,7},{9,8},{10,9},{11,1... | collective-permute-start | bytes 786440 | tf_op jit(solution)/shard_map/ppermute | solution.py:32
  38.3 13.3 %collective-permute-start.3 = (bf16[16,8192]{1,0:T(8,128)(2,1)S(1)}, bf16[16,8192]{1,0:T(8,128)(2,1)}, u32[]{:S(2)}, u32[]{:S(2)}) collective-permute-start(bf16[16,8192]{1,0:T(8,128)(2,1)S(1)} %divide_convert_fusion), channel_id=1, source_target_pairs={{2,0},{3,1},{4,2},{5,3},{6,4},{7,5},{8,6},{9,7},{10,8},{11,9},{12,... | collective-permute-start | bytes 786440 | tf_op jit(solution)/shard_map/ppermute | solution.py:32
  41.9 19.6 %collective-permute-start.4 = (bf16[16,8192]{1,0:T(8,128)(2,1)S(1)}, bf16[16,8192]{1,0:T(8,128)(2,1)}, u32[]{:S(2)}, u32[]{:S(2)}) collective-permute-start(bf16[16,8192]{1,0:T(8,128)(2,1)S(1)} %divide_convert_fusion), channel_id=1, source_target_pairs={{3,0},{4,1},{5,2},{6,3},{7,4},{8,5},{9,6},{10,7},{11,8},{12,9},{13... | collective-permute-start | bytes 786440 | tf_op jit(solution)/shard_map/ppermute | solution.py:32
  114.1 5.2 copy-start
  185.0 5.2 copy-start
  256.0 5.2 copy-start
  326.9 5.2 copy-start
  397.9 5.2 copy-start
  468.8 5.2 copy-start
  539.8 5.2 copy-start
  610.7 5.2 copy-start
where the time goes:
time: 643 us; the launch traced here: 637 us
  local copies, waits for them, and re-layouts  404 us (63%)
  matrix products  164 us (26%)
  starting transfers between devices  24.5 us (4%)
  other arithmetic  22.1 us (3%)
  waiting for transfers between devices  21.8 us (3%)
    broadcast_in_dim x16, local copies, waits for them, and re-layouts, toeplitz_tiles(): jnp.broadcast_to(widened[..., None, :], leading + (tile_len, 2 * tile_len...  230 us
    dot_general x64, matrix products, advance(): jnp.einsum('bpjkw,bikuw->bpiju', span[:, :, :, quarter:quarter + group],...  161 us
    while x24, local copies, waits for them, and re-layouts  81.5 us
    slice x8, local copies, waits for them, and re-layouts, toeplitz_tiles(): repeated.reshape(leading + (tile_len * (2 * tile_len + 1),))  65.1 us
    add x8, other arithmetic, advance(): return total + jnp.stack(parts, 4)  18.5 us
  transfers between devices with their start and end apart: 6, of which 4 were waited for; matrix products, arithmetic and copies ran while one was open for 1% of the time, Pallas kernels for 0%

commit v1 on v0

v1 whole, which is shorter than its diff:
```python
import math

import jax
import jax.numpy as jnp
from jax import lax
from jax.experimental import pallas as pl
from jax.experimental.pallas import tpu as pltpu
from jax.sharding import PartitionSpec as P

TAPS = 64
HALF_WIN = 256
LAG = 512
BLOCK = 16
PAIR_SPAN = 4
PAIRS = 2
T = 8192
KW = 8448
BW = KW + 896
KC = 2816


def extended_2(value, sides, width):
    for axis, dim in sides:
        devices, length = (lax.axis_size(axis), value.shape[dim])
        up = [(i, (i + 1) % devices) for i in range(devices - 1)]
        down = [(j, i) for i, j in up]
        last = lax.slice_in_dim(value, length - width, length, axis=dim)
        leading = lax.slice_in_dim(value, 0, width, axis=dim)
        before = lax.ppermute(last, axis, up)
        after = lax.ppermute(leading, axis, down)
        value = jnp.concatenate([before, value, after], axis=dim)
    return value


def from_behind(block, axis, distance):
    devices = range(lax.axis_size(axis))
    route = [(i - distance, i) for i in devices if i - distance in devices]
    return lax.ppermute(block, axis, route)


def band_matrix(taps, row_count):
    length = row_count + taps.shape[0]
    widened = jnp.concatenate([taps, jnp.zeros((row_count + 1,), taps.dtype)])
    repeated = jnp.broadcast_to(widened[None, :], (row_count, length + 1))
    return repeated.reshape(-1)[: row_count * length].reshape(row_count, length)


def running_level(magnitude):
    count, times = magnitude.shape
    width = 2 * HALF_WIN
    padded = jnp.pad(magnitude, ((0, 0), (HALF_WIN, HALF_WIN)))
    tiles = padded.reshape(count, times // width + 1, width)
    windows = jnp.concatenate([tiles[:, :-1], tiles[:, 1:]], -1)
    inner = jnp.arange(2 * width)[:, None]
    outer = jnp.arange(width)[None, :]
    boxcar = ((inner >= outer) & (inner <= outer + width)).astype(jnp.float32)
    summed = jnp.einsum(
        "cnx,xt->cnt",
        windows,
        boxcar,
        precision=lax.Precision.HIGHEST,
        preferred_element_type=jnp.float32,
    )
    return summed.reshape(count, times) / (width + 1)


def normalize(filtered):
    level = running_level(jnp.abs(filtered))
    return (filtered / (level + 1e-05)).astype(jnp.bfloat16)


def build_a(a32, a_sh):
    lane = lax.broadcasted_iota(jnp.int32,(8,128),1)
    sub = lax.broadcasted_iota(jnp.int32,(8,128),0)
    lo = lane >= sub
    hi = lane >= sub+8
    def col(u, prev):
        c0=pl.multiple_of(u*128,128)
        out=[]
        for i in range(16):
            x = jnp.broadcast_to(a32[i:i+1, pl.ds(c0,128)],(8,128))
            r0 = pltpu.roll(x,0,1,stride=1,stride_axis=0)
            r1 = pltpu.roll(x,8,1,stride=1,stride_axis=0)
            p0,p1=prev[i]
            y = jnp.concatenate([jnp.where(lo,r0,p0),jnp.where(hi,r1,p1)],0)
            a_sh[16*i:16*i+16, pl.ds(c0,128)] = y.astype(jnp.bfloat16)
            out.append((r0,r1))
        return tuple(out)
    z=jnp.zeros((8,128),jnp.float32)
    lax.fori_loop(0,KW//128,col,((z,z),)*16)

def build_b(bpad, b_sh):
    lane = lax.broadcasted_iota(jnp.int32,(32,128),1)
    def col(u,_):
        c0 = pl.multiple_of(u*128,128)
        x = bpad[:, pl.ds(c0,128)]
        y = bpad[:, pl.ds(pl.multiple_of(u*128+128,128),128)]
        b_sh[0:32, pl.ds(c0,128)] = x
        for q in range(1,8):
            s = 128-16*q
            w = jnp.where(lane < s, pltpu.roll(x.astype(jnp.float32),s,1), pltpu.roll(y.astype(jnp.float32),s,1))
            b_sh[32*q:32*q+32, pl.ds(c0,128)] = w.astype(jnp.bfloat16)
        return 0
    lax.fori_loop(0,BW//128,col,0,unroll=2)

def relayout(acc, o_ref, scale):
    lane = lax.broadcasted_iota(jnp.int32,(8,128),1)
    def one(g,_):
      qh=g
      for kj in range(8):
        k=kj//4; jh=(kj//2)%2; ih=kj%2
        xs=[acc[qh, 32*ql+k*16+jh*8:32*ql+k*16+jh*8+8, ih*128:ih*128+128]*scale for ql in range(8)]
        for b in (1,2,4):
            m = (lane//16)&b
            new=list(xs)
            for q in range(8):
                if q & b == 0:
                    x,y=xs[q],xs[q|b]
                    new[q]=jnp.where(m==0,x,pltpu.roll(y,16*b,1))
                    new[q|b]=jnp.where(m==0,pltpu.roll(x,128-16*b,1),y)
            xs=new
        for i in range(8):
            o_ref[k, ih*8+i, jh*8:jh*8+8, pl.ds(pl.multiple_of(qh*128,128),128)]=xs[i]
      return 0
    lax.fori_loop(0,8,one,0)

def kernel(pat, ext, o_ref, a32, a_sh, bpad, b_sh, acc):
    a32[:, :T] = ext[0:16, :].astype(jnp.float32)
    a32[:, T:] = jnp.zeros((16, KW - T), jnp.float32)
    build_a(a32, a_sh)
    bpad[:, :LAG] = jnp.zeros((32, LAG), jnp.bfloat16)
    bpad[:, LAG + T :] = jnp.zeros((32, BW + 128 - LAG - T), jnp.bfloat16)
    for k in range(PAIRS):
        first = pl.multiple_of(pat[0, k] * 16, 16)
        bpad[16 * k : 16 * k + 16, LAG : LAG + T] = ext[pl.ds(first, 16), :]
    build_b(bpad, b_sh)
    acc[...] = jnp.zeros_like(acc)

    def kouter(s, _):
        for qh in range(8):
            acc[qh] += lax.dot_general(
                b_sh[:, pl.ds(pl.multiple_of(s * KC + qh * 128, 128), KC)],
                a_sh[:, pl.ds(pl.multiple_of(s * KC, 128), KC)],
                (((1,), (1,)), ((), ())),
                preferred_element_type=jnp.float32,
            )
        return 0

    lax.fori_loop(0, KW // KC, kouter, 0)
    relayout(acc, o_ref, 1 / math.sqrt(T))


def correlate(pattern, ext):
    return pl.pallas_call(
        kernel,
        out_shape=jax.ShapeDtypeStruct((2, 16, 16, 1024), jnp.float32),
        in_specs=[
            pl.BlockSpec(memory_space=pltpu.SMEM),
            pl.BlockSpec(memory_space=pltpu.VMEM),
        ],
        out_specs=pl.BlockSpec(memory_space=pltpu.VMEM),
        scratch_shapes=[
            pltpu.VMEM((16, KW), jnp.float32),
            pltpu.VMEM((256, KW), jnp.bfloat16),
            pltpu.VMEM((32, BW + 128), jnp.bfloat16),
            pltpu.VMEM((256, BW), jnp.bfloat16),
            pltpu.VMEM((8, 256, 256), jnp.float32),
        ],
        compiler_params=pltpu.CompilerParams(vmem_limit_bytes=48 << 20),
        name="corr",
    )(pattern, ext)


def body(record, alive, taps, pattern):
    row_count, time_span = record.shape
    tm_count = lax.axis_size("tm")
    mine_count = row_count // tm_count
    reach_rows = (PAIR_SPAN - 1) * BLOCK
    lively = alive.astype(jnp.float32)[:, None]
    masked = record * lively
    rimmed = extended_2(masked, (("chan", 0),), TAPS // 2)
    filtered = lively * jnp.dot(
        band_matrix(taps, row_count),
        rimmed,
        precision=lax.Precision.HIGHEST,
        preferred_element_type=jnp.float32,
    )
    whole = lax.all_to_all(filtered, "tm", split_axis=0, concat_axis=1, tiled=True)
    normed = normalize(whole)
    needed = -(-reach_rows // mine_count)
    pieces = [normed]
    for step in range(1, needed + 1):
        pieces.append(from_behind(normed, ("chan", "tm"), -step))
    extended = jnp.concatenate(pieces, 0)
    return correlate(pattern, extended)[None]


def solution(mesh):
    placed = (P("chan", "tm"), P("chan"), P(), P(("chan", "tm"), None))
    return jax.shard_map(
        body,
        mesh=mesh,
        in_specs=placed,
        out_specs=P(("chan", "tm"), None, None, None, None),
        check_vma=False,
    )
```

time: 643 us -> 80.7 us (0.13)
  the two profiles are of different devices: /device:TPU:168 before, /device:TPU:97 now
where the time goes in v1:
time: 80.7 us; the launch traced here: 80.3 us
  Pallas kernels  26.3 us (33%)
  waiting for transfers between devices  25 us (31%)
  starting transfers between devices  22.5 us (28%)
  matrix products  2.68 us (3%)
  other arithmetic  1.99 us (2%)
  local copies, waits for them, and re-layouts  1.73 us (2%)
    pallas_call x1, Pallas kernels, correlate(): pl.pallas_call(kernel, out_shape=jax.ShapeDtypeStruct((2, 16, 16, 1024),...  26.3 us
    ppermute x3, starting transfers between devices, from_behind(): return lax.ppermute(block, axis, route)  11.2 us
    ppermute x3, waiting for transfers between devices, from_behind(): return lax.ppermute(block, axis, route)  11 us
    all_to_all x1, waiting for transfers between devices, body(): lax.all_to_all(filtered, 'tm', split_axis=0, concat_axis=1, tiled=True)  9.23 us
    ppermute x1, starting transfers between devices, extended_2(): before = lax.ppermute(last, axis, up)  5.21 us
    ppermute x1, waiting for transfers between devices, extended_2(): after = lax.ppermute(leading, axis, down)  4.74 us
    all_to_all x1, starting transfers between devices, body(): lax.all_to_all(filtered, 'tm', split_axis=0, concat_axis=1, tiled=True)  4.22 us
    ppermute x1, starting transfers between devices, extended_2(): after = lax.ppermute(leading, axis, down)  1.92 us
  transfers between devices with their start and end apart: 6, of which 4 were waited for; matrix products, arithmetic and copies ran while one was open for 1% of the time, Pallas kernels for 0%

profile of v1, /device:TPU:97, one launch (start us, length us, event | category | flops | bytes accessed | tf_op | source)
XLA Modules:
  0.0 80.3 jit_solution(6538201034665749020)
XLA Ops:
  0.0 0.7 convert_element_type.9
  0.7 1.1 %broadcast_multiply_fusion = f32[128,1024]{1,0:T(8,128)S(1)} fusion(f32[128,1024]{1,0:T(8,128)} %param.4, f32[128]{0:T(128)S(1)} %convert_element_type.9), kind=kLoop, calls=%fused_computation.19 | loop fusion | flops 131072 | bytes 1049088 | tf_op jit(solution)/shard_map/mul | solution.py:180
  1.8 5.2 %collective-permute-start = (f32[32,1024]{1,0:T(8,128)S(1)}, f32[32,1024]{1,0:T(8,128)S(1)}, u32[]{:S(2)}, u32[]{:S(2)}) collective-permute-start(f32[32,1024]{1,0:T(8,128)S(1)} %get-tuple-element.7), channel_id=1, source_target_pairs={{0,8},{8,16},{16,24},{24,32},{32,40},{40,48},{48,56},{56,64},{64,7... | collective-permute-start | bytes 393224 | tf_op jit(solution)/shard_map/ppermute | solution.py:29
  7.1 1.9 %collective-permute-start.1 = (f32[32,1024]{1,0:T(8,128)S(1)}, f32[32,1024]{1,0:T(8,128)S(1)}, u32[]{:S(2)}, u32[]{:S(2)}) collective-permute-start(f32[32,1024]{1,0:T(8,128)S(1)} %get-tuple-element.8), channel_id=1, source_target_pairs={{8,0},{16,8},{24,16},{32,24},{40,32},{48,40},{56,48},{64,56},{72,6... | collective-permute-start | bytes 393224 | tf_op jit(solution)/shard_map/ppermute | solution.py:30
  9.0 0.7 concatenate.12
  9.7 0.3 reshape.24
  10.0 0.1 reshape.25
  10.1 0.0 collective-permute-done
  10.1 4.7 %collective-permute-done.1 = f32[32,1024]{1,0:T(8,128)S(1)} collective-permute-done((f32[32,1024]{1,0:T(8,128)S(1)}, f32[32,1024]{1,0:T(8,128)S(1)}, u32[]{:S(2)}, u32[]{:S(2)}) %collective-permute-start.1) | collective-permute-done | bytes 131104 | tf_op jit(solution)/shard_map/ppermute | solution.py:30
  14.8 1.4 %convolution_multiply_fusion = f32[128,1024]{1,0:T(8,128)} fusion(f32[128,192]{1,0:T(8,128)S(1)} %reshape.25, f32[32,1024]{1,0:T(8,128)S(1)} %collective-permute-done.1, f32[128,1024]{1,0:T(8,128)S(1)} %broadcast_multiply_fusion, f32[32,1024]{1,0:T(8,128)S(1)} %collective-permute-done, f32[128]{0:T(128)S(1)} %convert_element_type.9), kind=kOutput, calls=%fused_computation.7 | convolution fusion | flops 302514176 | bytes 1409536 | tf_op jit(solution)/shard_map/dot_general | solution.py:182
  16.3 4.2 %all-to-all-start = ((f32[8,16,1024]{2,1,0:T(8,128)}), f32[8,16,1024]{2,1,0:T(8,128)S(1)}, u32[]{:S(2)}, u32[]{:S(2)}) async-start(f32[8,16,1024]{2,1,0:T(8,128)} %bitcast), calls=%async_computation | async-start | bytes 1048576 | tf_op jit(solution)/shard_map/all_to_all | solution.py:188
  20.5 9.2 %all-to-all-done = f32[8,16,1024]{2,1,0:T(8,128)S(1)} async-done(((f32[8,16,1024]{2,1,0:T(8,128)}), f32[8,16,1024]{2,1,0:T(8,128)S(1)}, u32[]{:S(2)}, u32[]{:S(2)}) %all-to-all-start) | async-done | bytes 524320 | tf_op jit(solution)/shard_map/all_to_all | solution.py:188
  29.9 0.1 reshape.26
  30.0 0.1 fusion.21
  30.1 1.3 %fusion.7 = f32[16,16,512]{2,1,0:T(8,128)S(1)} fusion(f32[16,16,512]{2,1,0:T(8,128)S(1)} %get-tuple-element.6, f32[16,16,512]{2,1,0:T(8,128)S(1)} %get-tuple-element.5, s32[512]{0:T(512)S(1)} %iota_add_fusion), kind=kOutput, calls=%fused_computation.6 | convolution fusion | flops 1612709888 | bytes 1574912 | tf_op jit(solution)/shard_map/cnx,xt->cnt/dot_general | solution.py:57
  31.4 0.0 copy-start
  31.4 0.3 copy.9
  31.7 0.1 divide_convert_fusion
  31.8 3.9 %collective-permute-start.4 = (bf16[16,8192]{1,0:T(8,128)(2,1)S(1)}, bf16[16,8192]{1,0:T(8,128)(2,1)S(1)}, u32[]{:S(2)}, u32[]{:S(2)}) collective-permute-start(bf16[16,8192]{1,0:T(8,128)(2,1)S(1)} %divide_convert_fusion), channel_id=1, source_target_pairs={{3,0},{4,1},{5,2},{6,3},{7,4},{8,5},{9,6},{10,7},{11,8},{12,9},{13... | collective-permute-start | bytes 786440 | tf_op jit(solution)/shard_map/ppermute | solution.py:38
  35.7 4.0 %collective-permute-start.3 = (bf16[16,8192]{1,0:T(8,128)(2,1)S(1)}, bf16[16,8192]{1,0:T(8,128)(2,1)S(1)}, u32[]{:S(2)}, u32[]{:S(2)}) collective-permute-start(bf16[16,8192]{1,0:T(8,128)(2,1)S(1)} %divide_convert_fusion), channel_id=1, source_target_pairs={{2,0},{3,1},{4,2},{5,3},{6,4},{7,5},{8,6},{9,7},{10,8},{11,9},{12,... | collective-permute-start | bytes 786440 | tf_op jit(solution)/shard_map/ppermute | solution.py:38
  39.8 3.2 %collective-permute-start.2 = (bf16[16,8192]{1,0:T(8,128)(2,1)S(1)}, bf16[16,8192]{1,0:T(8,128)(2,1)S(1)}, u32[]{:S(2)}, u32[]{:S(2)}) collective-permute-start(bf16[16,8192]{1,0:T(8,128)(2,1)S(1)} %divide_convert_fusion), channel_id=1, source_target_pairs={{1,0},{2,1},{3,2},{4,3},{5,4},{6,5},{7,6},{8,7},{9,8},{10,9},{11,1... | collective-permute-start | bytes 786440 | tf_op jit(solution)/shard_map/ppermute | solution.py:38
  43.0 0.0 collective-permute-done.4
  43.0 6.7 %collective-permute-done.3 = bf16[16,8192]{1,0:T(8,128)(2,1)S(1)} collective-permute-done((bf16[16,8192]{1,0:T(8,128)(2,1)S(1)}, bf16[16,8192]{1,0:T(8,128)(2,1)S(1)}, u32[]{:S(2)}, u32[]{:S(2)}) %collective-permute-start.3) | collective-permute-done | bytes 262176 | tf_op jit(solution)/shard_map/ppermute | solution.py:38
  49.8 4.2 %collective-permute-done.2 = bf16[16,8192]{1,0:T(8,128)(2,1)S(1)} collective-permute-done((bf16[16,8192]{1,0:T(8,128)(2,1)S(1)}, bf16[16,8192]{1,0:T(8,128)(2,1)S(1)}, u32[]{:S(2)}, u32[]{:S(2)}) %collective-permute-start.2) | collective-permute-done | bytes 262176 | tf_op jit(solution)/shard_map/ppermute | solution.py:38
  54.0 0.1 pad_maximum_fusion.ext
  54.1 0.0 copy-done
  54.1 26.3 %corr.1 = f32[2,16,16,1024]{3,2,1,0:T(8,128)} custom-call(s32[1,2]{1,0:T(1,128)S(1)} %copy-done, bf16[64,8192]{1,0:T(8,128)(2,1)S(1)} %pad_maximum_fusion.ext), custom_call_target="tpu_custom_call" | custom-call | tf_op jit(solution)/shard_map/corr/pallas_call | solution.py:154
  (7 shorter events, 0.2 us)
Async XLA Ops:
  1.8 8.3 %collective-permute-start = (f32[32,1024]{1,0:T(8,128)S(1)}, f32[32,1024]{1,0:T(8,128)S(1)}, u32[]{:S(2)}, u32[]{:S(2)}) collective-permute-start(f32[32,1024]{1,0:T(8,128)S(1)} %get-tuple-element.7), channel_id=1, source_target_pairs={{0,8},{8,16},{16,24},{24,32},{32,40},{40,48},{48,56},{56,64},{64,7... | collective-permute-start | bytes 393224 | tf_op jit(solution)/shard_map/ppermute | solution.py:29
  7.1 7.8 %collective-permute-start.1 = (f32[32,1024]{1,0:T(8,128)S(1)}, f32[32,1024]{1,0:T(8,128)S(1)}, u32[]{:S(2)}, u32[]{:S(2)}) collective-permute-start(f32[32,1024]{1,0:T(8,128)S(1)} %get-tuple-element.8), channel_id=1, source_target_pairs={{8,0},{16,8},{24,16},{32,24},{40,32},{48,40},{56,48},{64,56},{72,6... | collective-permute-start | bytes 393224 | tf_op jit(solution)/shard_map/ppermute | solution.py:30
  16.3 13.5 %all-to-all-start = ((f32[8,16,1024]{2,1,0:T(8,128)}), f32[8,16,1024]{2,1,0:T(8,128)S(1)}, u32[]{:S(2)}, u32[]{:S(2)}) async-start(f32[8,16,1024]{2,1,0:T(8,128)} %bitcast), calls=%async_computation | async-start | bytes 1048576 | tf_op jit(solution)/shard_map/all_to_all | solution.py:188
  31.4 22.7 %copy-start = (s32[1,2]{1,0:T(1,128)S(1)}, s32[1,2]{1,0:T(1,128)}, u32[]{:S(2)}) copy-start(s32[1,2]{1,0:T(1,128)} %pat.1) | copy-start | bytes 28
  31.8 11.2 %collective-permute-start.4 = (bf16[16,8192]{1,0:T(8,128)(2,1)S(1)}, bf16[16,8192]{1,0:T(8,128)(2,1)S(1)}, u32[]{:S(2)}, u32[]{:S(2)}) collective-permute-start(bf16[16,8192]{1,0:T(8,128)(2,1)S(1)} %divide_convert_fusion), channel_id=1, source_target_pairs={{3,0},{4,1},{5,2},{6,3},{7,4},{8,5},{9,6},{10,7},{11,8},{12,9},{13... | collective-permute-start | bytes 786440 | tf_op jit(solution)/shard_map/ppermute | solution.py:38
  35.7 14.0 %collective-permute-start.3 = (bf16[16,8192]{1,0:T(8,128)(2,1)S(1)}, bf16[16,8192]{1,0:T(8,128)(2,1)S(1)}, u32[]{:S(2)}, u32[]{:S(2)}) collective-permute-start(bf16[16,8192]{1,0:T(8,128)(2,1)S(1)} %divide_convert_fusion), channel_id=1, source_target_pairs={{2,0},{3,1},{4,2},{5,3},{6,4},{7,5},{8,6},{9,7},{10,8},{11,9},{12,... | collective-permute-start | bytes 786440 | tf_op jit(solution)/shard_map/ppermute | solution.py:38
  39.8 14.2 %collective-permute-start.2 = (bf16[16,8192]{1,0:T(8,128)(2,1)S(1)}, bf16[16,8192]{1,0:T(8,128)(2,1)S(1)}, u32[]{:S(2)}, u32[]{:S(2)}) collective-permute-start(bf16[16,8192]{1,0:T(8,128)(2,1)S(1)} %divide_convert_fusion), channel_id=1, source_target_pairs={{1,0},{2,1},{3,2},{4,3},{5,4},{6,5},{7,6},{8,7},{9,8},{10,9},{11,1... | collective-permute-start | bytes 786440 | tf_op jit(solution)/shard_map/ppermute | solution.py:38

commit v2 on v1

v2 whole, which is shorter than its diff:
```python
import math

import jax
import jax.numpy as jnp
from jax import lax
from jax.experimental import pallas as pl
from jax.experimental.pallas import tpu as pltpu
from jax.sharding import PartitionSpec as P

TAPS = 64
HALF_WIN = 256
LAG = 512
BLOCK = 16
PAIR_SPAN = 4
PAIRS = 2
T = 8192
KW = 8448
BW = KW + 896
KC = 2816


TM = 8
MESH = pl.DeviceIdType.MESH
DIRS = [(dc, dt) for dc in (-1, 0, 1) for dt in (-1, 0, 1) if (dc, dt) != (0, 0)]
ROWS = {-1: (32, 160, 32), 0: (32, 32, 128), 1: (128, 0, 32)}
COLS = {-1: (256, 1280, 256), 0: (256, 256, 1024), 1: (1024, 0, 256)}


def front_kernel(
    rec, alive, taps, pat, out, rim, nbuf, pack, pats,
    halo_send, halo_recv, pat_send, pat_recv, up_send, up_recv, send_sem, recv_sem,
):
    c = lax.axis_index("chan")
    t = lax.axis_index("tm")
    chans = lax.axis_size("chan")

    def inside(dc, dt):
        ok = jnp.bool_(True)
        if dc == -1:
            ok = ok & (c > 0)
        if dc == 1:
            ok = ok & (c < chans - 1)
        if dt == -1:
            ok = ok & (t > 0)
        if dt == 1:
            ok = ok & (t < TM - 1)
        return ok

    barrier = pltpu.get_barrier_semaphore()
    for d in range(1, TM):
        pl.semaphore_signal(barrier, inc=1, device_id=(c, lax.rem(t + d, TM)), device_id_type=MESH)
    for dc, dt in DIRS:
        if dc != 0:
            @pl.when(inside(dc, dt))
            def _():
                pl.semaphore_signal(barrier, inc=1, device_id=(c + dc, t + dt), device_id_type=MESH)

    eye = lax.broadcasted_iota(jnp.int32, (128, 128), 0) == lax.broadcasted_iota(jnp.int32, (128, 128), 1)
    row = jnp.broadcast_to(alive[...].astype(jnp.float32), (128, 128))
    lively = jnp.sum(jnp.where(eye, row, 0.0), axis=1, keepdims=True)
    rim[32:160, 256:1280] = rec[...] * lively
    pats[t, 0:8, :] = jnp.full((8, 128), pat[0, 0], jnp.int32)
    pats[t, 8:16, :] = jnp.full((8, 128), pat[0, 1], jnp.int32)

    @pl.when(c == 0)
    def _():
        rim[0:32, :] = jnp.zeros((32, 1536), jnp.float32)

    @pl.when(c == chans - 1)
    def _():
        rim[160:192, :] = jnp.zeros((32, 1536), jnp.float32)
        nbuf[128:176, :] = jnp.zeros((48, 1024), jnp.bfloat16)

    @pl.when(t == 0)
    def _():
        rim[:, 0:256] = jnp.zeros((192, 256), jnp.float32)

    @pl.when(t == TM - 1)
    def _():
        rim[:, 1280:1536] = jnp.zeros((192, 256), jnp.float32)

    peers = TM - 1 + jnp.where(c > 0, 1, 0) * (3 - jnp.where(t == 0, 1, 0) - jnp.where(t == TM - 1, 1, 0))
    peers = peers + jnp.where(c < chans - 1, 1, 0) * (3 - jnp.where(t == 0, 1, 0) - jnp.where(t == TM - 1, 1, 0))
    pl.semaphore_wait(barrier, peers)

    def halo(e, dc, dt, away=1):
        rs, rt, rn = ROWS[dc]
        cs, ct, cn = COLS[dt]
        return pltpu.make_async_remote_copy(
            src_ref=rim.at[pl.ds(rs, rn), pl.ds(cs, cn)],
            dst_ref=rim.at[pl.ds(rt, rn), pl.ds(ct, cn)],
            send_sem=halo_send.at[e], recv_sem=halo_recv.at[e],
            device_id=(c + away * dc, t + away * dt), device_id_type=MESH,
        )

    for e, (dc, dt) in enumerate(DIRS):
        @pl.when(inside(dc, dt))
        def _():
            halo(e, dc, dt).start()

    def pat_copy(d):
        return pltpu.make_async_remote_copy(
            src_ref=pats.at[t], dst_ref=pats.at[t], send_sem=pat_send.at[d], recv_sem=pat_recv.at[t],
            device_id=(c, lax.rem(t + d, TM)), device_id_type=MESH,
        )

    for d in range(1, TM):
        pat_copy(d).start()

    wide = jnp.concatenate([taps[...], jnp.zeros((1, 192), jnp.float32)], 1)
    band = pltpu.roll(jnp.broadcast_to(wide, (128, 256)), 0, 1, stride=1, stride_axis=0)[:, 0:192]
    inner = lax.broadcasted_iota(jnp.int32, (768, 256), 0)
    outer = lax.broadcasted_iota(jnp.int32, (768, 256), 1)
    boxcar = jnp.where((inner >= outer) & (inner <= outer + 512), 1.0, 0.0).astype(jnp.bfloat16)

    for e, (dc, dt) in enumerate(DIRS):
        @pl.when(inside(-dc, -dt))
        def _():
            halo(e, dc, dt, -1).wait_recv()

    filtered = lively * jnp.dot(
        band, rim[...], precision=lax.Precision.HIGHEST, preferred_element_type=jnp.float32
    )
    size = jnp.abs(filtered)
    high = size.astype(jnp.bfloat16)
    rest = size - high.astype(jnp.float32)
    mid = rest.astype(jnp.bfloat16)
    low = (rest - mid.astype(jnp.float32)).astype(jnp.bfloat16)
    for b in range(4):
        total = None
        for part in (high, mid, low):
            s = jnp.dot(part[:, 256 * b : 256 * b + 768], boxcar, preferred_element_type=jnp.float32)
            total = s if total is None else total + s
        level = total / (2 * HALF_WIN + 1)
        mine = filtered[:, 256 * b + 256 : 256 * b + 512]
        nbuf[0:128, 256 * b : 256 * b + 256] = (mine / (level + 1e-5)).astype(jnp.bfloat16)

    def up():
        return pltpu.make_async_remote_copy(
            src_ref=nbuf.at[pl.ds(0, 48), :], dst_ref=nbuf.at[pl.ds(128, 48), :],
            send_sem=up_send, recv_sem=up_recv, device_id=(c - 1, t), device_id_type=MESH,
        )

    @pl.when(c > 0)
    def _():
        up().start()

    def fill(dest, to):
        first = pl.multiple_of(dest * 16, 16)
        for j in range(8):
            cols = slice(128 * j, 128 * j + 128)
            blocks = [nbuf[pl.ds(pl.multiple_of(first + 16 * o, 16), 16), cols] for o in range(4)]
            to[0:16, cols] = blocks[0]
            for k in range(PAIRS):
                offset = pats[dest, 8 * k : 8 * k + 8, :]
                offset = jnp.concatenate([offset, offset], 0)
                chosen = None
                for o in range(4):
                    term = blocks[o].astype(jnp.float32)
                    chosen = term if o == 0 else jnp.where(offset == o, term, chosen)
                to[16 * k + 16 : 16 * k + 32, cols] = chosen.astype(jnp.bfloat16)

    def deliver(d):
        dest = lax.rem(t + d, TM)
        return pltpu.make_async_remote_copy(
            src_ref=pack.at[d], dst_ref=out.at[t], send_sem=send_sem.at[d], recv_sem=recv_sem.at[t],
            device_id=(c, dest), device_id_type=MESH,
        )

    for d in range(1, TM):
        src = lax.rem(t + d, TM)
        pltpu.make_async_remote_copy(
            src_ref=pats.at[src], dst_ref=pats.at[src], send_sem=pat_send.at[d], recv_sem=pat_recv.at[src],
            device_id=(c, src), device_id_type=MESH,
        ).wait_recv()

    for last in (False, True):
        if last:
            @pl.when(c < chans - 1)
            def _():
                up().wait_recv()
        for d in list(range(1, TM)) + [0]:
            dest = lax.rem(t + d, TM)
            @pl.when((dest >= 5) if last else (dest < 5))
            def _():
                if d == 0:
                    fill(dest, out.at[t])
                else:
                    fill(dest, pack.at[d])
                    deliver(d).start()

    for d in range(1, TM):
        src = lax.rem(t + d, TM)
        pltpu.make_async_remote_copy(
            src_ref=pack.at[d], dst_ref=out.at[src], send_sem=send_sem.at[d], recv_sem=recv_sem.at[src],
            device_id=(c, src), device_id_type=MESH,
        ).wait_recv()
    for d in range(1, TM):
        deliver(d).wait_send()
        pat_copy(d).wait_send()
    for e, (dc, dt) in enumerate(DIRS):
        @pl.when(inside(dc, dt))
        def _():
            halo(e, dc, dt).wait_send()

    @pl.when(c > 0)
    def _():
        up().wait_send()


def front(record, alive, taps, pattern):
    dma = pltpu.SemaphoreType.DMA
    return pl.pallas_call(
        front_kernel,
        out_shape=jax.ShapeDtypeStruct((TM, 48, 1024), jnp.bfloat16),
        in_specs=[pl.BlockSpec(memory_space=pltpu.VMEM)] * 3 + [pl.BlockSpec(memory_space=pltpu.SMEM)],
        out_specs=pl.BlockSpec(memory_space=pltpu.VMEM),
        scratch_shapes=[
            pltpu.VMEM((192, 1536), jnp.float32),
            pltpu.VMEM((176, 1024), jnp.bfloat16),
            pltpu.VMEM((TM, 48, 1024), jnp.bfloat16),
            pltpu.VMEM((TM, 16, 128), jnp.int32),
            dma((8,)), dma((8,)), dma((TM,)), dma((TM,)), dma(()), dma(()), dma((TM,)), dma((TM,)),
        ],
        compiler_params=pltpu.CompilerParams(
            collective_id=0, has_side_effects=True, vmem_limit_bytes=32 << 20
        ),
        name="front",
    )(record, alive.reshape(1, 128), taps.reshape(1, 64), pattern)


def build_a(a32, a_sh):
    lane = lax.broadcasted_iota(jnp.int32,(8,128),1)
    sub = lax.broadcasted_iota(jnp.int32,(8,128),0)
    lo = lane >= sub
    hi = lane >= sub+8
    def col(u, prev):
        c0=pl.multiple_of(u*128,128)
        out=[]
        for i in range(16):
            x = jnp.broadcast_to(a32[i:i+1, pl.ds(c0,128)],(8,128))
            r0 = pltpu.roll(x,0,1,stride=1,stride_axis=0)
            r1 = pltpu.roll(x,8,1,stride=1,stride_axis=0)
            p0,p1=prev[i]
            y = jnp.concatenate([jnp.where(lo,r0,p0),jnp.where(hi,r1,p1)],0)
            a_sh[16*i:16*i+16, pl.ds(c0,128)] = y.astype(jnp.bfloat16)
            out.append((r0,r1))
        return tuple(out)
    z=jnp.zeros((8,128),jnp.float32)
    lax.fori_loop(0,KW//128,col,((z,z),)*16)

def build_b(bpad, b_sh):
    lane = lax.broadcasted_iota(jnp.int32,(32,128),1)
    def col(u,_):
        c0 = pl.multiple_of(u*128,128)
        x = bpad[:, pl.ds(c0,128)]
        y = bpad[:, pl.ds(pl.multiple_of(u*128+128,128),128)]
        b_sh[0:32, pl.ds(c0,128)] = x
        for q in range(1,8):
            s = 128-16*q
            w = jnp.where(lane < s, pltpu.roll(x.astype(jnp.float32),s,1), pltpu.roll(y.astype(jnp.float32),s,1))
            b_sh[32*q:32*q+32, pl.ds(c0,128)] = w.astype(jnp.bfloat16)
        return 0
    lax.fori_loop(0,BW//128,col,0,unroll=2)

def relayout(acc, o_ref, scale):
    lane = lax.broadcasted_iota(jnp.int32,(8,128),1)
    def one(g,_):
      qh=g
      for kj in range(8):
        k=kj//4; jh=(kj//2)%2; ih=kj%2
        xs=[acc[qh, 32*ql+k*16+jh*8:32*ql+k*16+jh*8+8, ih*128:ih*128+128]*scale for ql in range(8)]
        for b in (1,2,4):
            m = (lane//16)&b
            new=list(xs)
            for q in range(8):
                if q & b == 0:
                    x,y=xs[q],xs[q|b]
                    new[q]=jnp.where(m==0,x,pltpu.roll(y,16*b,1))
                    new[q|b]=jnp.where(m==0,pltpu.roll(x,128-16*b,1),y)
            xs=new
        for i in range(8):
            o_ref[k, ih*8+i, jh*8:jh*8+8, pl.ds(pl.multiple_of(qh*128,128),128)]=xs[i]
      return 0
    lax.fori_loop(0,8,one,0)

def kernel(ext, o_ref, a32, a_sh, bpad, b_sh, acc):
    for s in range(8):
        a32[:, 1024 * s : 1024 * s + 1024] = ext[s, 0:16, :].astype(jnp.float32)
    a32[:, T:] = jnp.zeros((16, KW - T), jnp.float32)
    build_a(a32, a_sh)
    bpad[:, :LAG] = jnp.zeros((32, LAG), jnp.bfloat16)
    bpad[:, LAG + T :] = jnp.zeros((32, BW + 128 - LAG - T), jnp.bfloat16)
    for s in range(8):
        bpad[:, LAG + 1024 * s : LAG + 1024 * s + 1024] = ext[s, 16:48, :]
    build_b(bpad, b_sh)
    acc[...] = jnp.zeros_like(acc)

    def kouter(s, _):
        for qh in range(8):
            acc[qh] += lax.dot_general(
                b_sh[:, pl.ds(pl.multiple_of(s * KC + qh * 128, 128), KC)],
                a_sh[:, pl.ds(pl.multiple_of(s * KC, 128), KC)],
                (((1,), (1,)), ((), ())),
                preferred_element_type=jnp.float32,
            )
        return 0

    lax.fori_loop(0, KW // KC, kouter, 0)
    relayout(acc, o_ref, 1 / math.sqrt(T))


def correlate(ext):
    return pl.pallas_call(
        kernel,
        out_shape=jax.ShapeDtypeStruct((2, 16, 16, 1024), jnp.float32),
        in_specs=[
            pl.BlockSpec(memory_space=pltpu.VMEM),
        ],
        out_specs=pl.BlockSpec(memory_space=pltpu.VMEM),
        scratch_shapes=[
            pltpu.VMEM((16, KW), jnp.float32),
            pltpu.VMEM((256, KW), jnp.bfloat16),
            pltpu.VMEM((32, BW + 128), jnp.bfloat16),
            pltpu.VMEM((256, BW), jnp.bfloat16),
            pltpu.VMEM((8, 256, 256), jnp.float32),
        ],
        compiler_params=pltpu.CompilerParams(vmem_limit_bytes=48 << 20),
        name="corr",
    )(ext)


def body(record, alive, taps, pattern):
    return correlate(front(record, alive, taps, pattern))[None]


def solution(mesh):
    placed = (P("chan", "tm"), P("chan"), P(), P(("chan", "tm"), None))
    return jax.shard_map(
        body,
        mesh=mesh,
        in_specs=placed,
        out_specs=P(("chan", "tm"), None, None, None, None),
        check_vma=False,
    )
```

time: 80.7 us -> 57.5 us (0.71)
  the two profiles are of different devices: /device:TPU:97 before, /device:TPU:127 now
where the time goes in v2:
time: 57.5 us; the launch traced here: 56.4 us
  Pallas kernels  53.4 us (93%)
  local copies, waits for them, and re-layouts  3.01 us (5%)
    pallas_call x1, Pallas kernels, front(): pl.pallas_call(front_kernel, out_shape=jax.ShapeDtypeStruct((TM, 48, 1024...  27.7 us
    pallas_call x1, Pallas kernels, correlate(): pl.pallas_call(kernel, out_shape=jax.ShapeDtypeStruct((2, 16, 16, 1024),...  25.7 us
    unnamed x8, local copies, waits for them, and re-layouts  3.01 us

profile of v2, /device:TPU:127, one launch (start us, length us, event | category | flops | bytes accessed | tf_op | source)
XLA Modules:
  0.0 56.4 jit_solution(17166771865624089234)
XLA Ops:
  0.0 0.0 copy-start
  0.0 1.0 %copy-done = f32[128,1024]{1,0:T(8,128)S(1)} copy-done((f32[128,1024]{1,0:T(8,128)S(1)}, f32[128,1024]{1,0:T(8,128)}, u32[]{:S(2)}) %copy-start) | copy-done | bytes 524312
  1.0 0.0 copy-start.1
  1.0 0.7 %copy-done.1 = s32[128]{0:T(128)S(1)} copy-done((s32[128]{0:T(128)S(1)}, s32[128]{0:T(128)}, u32[]{:S(2)}) %copy-start.1) | copy-done | bytes 536
  1.7 0.0 copy-start.2
  1.7 0.7 %copy-done.2 = f32[64]{0:T(128)S(1)} copy-done((f32[64]{0:T(128)S(1)}, f32[64]{0:T(128)}, u32[]{:S(2)}) %copy-start.2) | copy-done | bytes 280
  2.4 0.0 copy-start.3
  2.4 0.7 %copy-done.3 = s32[1,2]{1,0:T(1,128)S(1)} copy-done((s32[1,2]{1,0:T(1,128)S(1)}, s32[1,2]{1,0:T(1,128)}, u32[]{:S(2)}) %copy-start.3) | copy-done | bytes 32
  3.0 27.7 %front.1.ext = bf16[8,48,1024]{2,1,0:T(8,128)(2,1)S(1)} custom-call(f32[128,1024]{1,0:T(8,128)S(1)} %copy-done, s32[1,128]{1,0:T(1,128)S(1)} %bitcast.3, f32[1,64]{1,0:T(1,128)S(1)} %bitcast.4, s32[1,2]{1,0:T(1,128)S(1)} %copy-done.3), custom_call_target="tpu_custom_call" | custom-call | tf_op jit(solution)/shard_map/front/pallas_call | solution.py:213
  30.7 25.7 %corr.1 = f32[2,16,16,1024]{3,2,1,0:T(8,128)} custom-call(bf16[8,48,1024]{2,1,0:T(8,128)(2,1)S(1)} %front.1.ext), custom_call_target="tpu_custom_call" | custom-call | tf_op jit(solution)/shard_map/corr/pallas_call | solution.py:314
Async XLA Ops:
  0.0 1.0 %copy-start = (f32[128,1024]{1,0:T(8,128)S(1)}, f32[128,1024]{1,0:T(8,128)}, u32[]{:S(2)}) copy-start(f32[128,1024]{1,0:T(8,128)} %rec.1) | copy-start | bytes 1572868
  1.0 0.7 %copy-start.1 = (s32[128]{0:T(128)S(1)}, s32[128]{0:T(128)}, u32[]{:S(2)}) copy-start(s32[128]{0:T(128)} %param.5) | copy-start | bytes 1540
  1.7 0.7 %copy-start.2 = (f32[64]{0:T(128)S(1)}, f32[64]{0:T(128)}, u32[]{:S(2)}) copy-start(f32[64]{0:T(128)} %param.6) | copy-start | bytes 772
  2.4 0.7 %copy-start.3 = (s32[1,2]{1,0:T(1,128)S(1)}, s32[1,2]{1,0:T(1,128)}, u32[]{:S(2)}) copy-start(s32[1,2]{1,0:T(1,128)} %pat.1) | copy-start | bytes 28

commit v3 on v2

v3 whole, which is shorter than its diff:
```python
import functools
import math

import jax
import jax.numpy as jnp
from jax import lax
from jax.experimental import pallas as pl
from jax.experimental.pallas import tpu as pltpu
from jax.sharding import PartitionSpec as P

TAPS = 64
HALF_WIN = 256
LAG = 512
BLOCK = 16
PAIR_SPAN = 4
PAIRS = 2
T = 8192


TM = 8
MESH = pl.DeviceIdType.MESH
ORDER = [(0, 0), (0, 1), (0, 3), (1, 0), (0, 2), (1, 1), (1, 3), (1, 2)]


def peer(t, dx, dy):
    return (t // 4 + dx) % 2 * 4 + (t % 4 + dy) % 4


def schedule():
    steps, needs = [], []
    for t in range(TM):
        rank = {peer(t, *d): r for r, d in enumerate(ORDER)}
        need = {low: max(rank.get(low, 0), rank.get(low + 1, 0)) for low in range(-1, TM)}
        order = sorted(need, key=lambda low: (need[low], low))
        steps.append([low + 1 for low in order])
        needs.append([need[low] for low in order])
    return steps, needs


def pick(values, index):
    out = jnp.int32(values[0])
    for n in range(1, len(values)):
        out = jnp.where(index == n, jnp.int32(values[n]), out)
    return out


def look_up(table, t, n):
    packed = [sum(row[m] * 9**k for k, row in enumerate(table)) for m in range(len(table[0]))]
    return pick(packed, n) // pick([9**k for k in range(TM)], t) % 9


DIRS = [(dc, dt) for dc in (-1, 0, 1) for dt in (-1, 0, 1) if (dc, dt) != (0, 0)]
ROWS = {-1: (32, 160, 32), 0: (32, 32, 128), 1: (128, 0, 32)}
COLS = {-1: (256, 1280, 256), 0: (256, 256, 1024), 1: (1024, 0, 256)}


def accumulate(low, high, acc, own, near, far, out, last):
    lane = lax.broadcasted_iota(jnp.int32, (8, 128), 1)
    sub = lax.broadcasted_iota(jnp.int32, (8, 128), 0)
    near[:, 0:640] = low[0:16, 384:1024].astype(jnp.float32)
    near[:, 640:1152] = high[0:16, 0:512].astype(jnp.float32)
    for i in range(BLOCK):
        before = None
        for u in range(9):
            x = jnp.broadcast_to(near[i : i + 1, 128 * u : 128 * u + 128], (8, 128))
            now = [pltpu.roll(x, 8 * h, 1, stride=1, stride_axis=0) for h in range(2)]
            if u > 0:
                y = [jnp.where(lane >= sub + 8 * h, now[h], before[h]) for h in range(2)]
                own[16 * i : 16 * i + 16, 128 * u - 128 : 128 * u] = jnp.concatenate(y, 0).astype(jnp.bfloat16)
            before = now
    both = jnp.concatenate([low[16:48, :], high[16:48, :]], 1)
    for ql in range(8):
        far[32 * ql : 32 * ql + 32, :] = both[:, 16 * ql : 16 * ql + 1920]

    def product(qh):
        return lax.dot_general(
            far[:, pl.ds(pl.multiple_of(128 * qh, 128), 1024)],
            own[...],
            (((1,), (1,)), ((), ())),
            preferred_element_type=jnp.float32,
        )

    for qh in range(8):
        acc[qh] += product(qh)

    @pl.when(last)
    def _():
        lax.fori_loop(0, 8, functools.partial(transpose, acc, out), 0)


def transpose(acc, out, qh, _):
    group = lax.broadcasted_iota(jnp.int32, (8, 128), 1) // 16
    for k in range(PAIRS):
        for jh in range(2):
            for ih in range(2):
                first = 16 * k + 8 * jh
                xs = []
                for ql in range(8):
                    x = acc[qh, 32 * ql + first : 32 * ql + first + 8, 128 * ih : 128 * ih + 128] * (1.0 / math.sqrt(T))
                    xs.append(pltpu.roll(x, 16 * ql, 1) if ql else x)
                xs = [xs[-m % 8] for m in range(8)]
                for bit in (1, 2, 4):
                    moved = group & bit != 0
                    xs = [jnp.where(moved, xs[(m - bit) % 8], xs[m]) for m in range(8)]
                for i in range(8):
                    y = pltpu.roll(xs[i], 128 - 16 * i, 1) if i else xs[i]
                    out[k, 8 * ih + i, 8 * jh : 8 * jh + 8, pl.ds(pl.multiple_of(128 * qh, 128), 128)] = y
    return 0


def front_kernel(
    rec_any, alive_any, taps_any, pat_any, out, acc, rec, alive, taps, pat, rim, nbuf, pack, pats, slots, own, near, far, filtered, sizes,
    arg_sem, halo_send, halo_recv, pat_send, pat_recv, up_send, up_recv, send_sem, recv_sem,
):
    c = lax.axis_index("chan")
    t = lax.axis_index("tm")
    chans = lax.axis_size("chan")

    def inside(dc, dt):
        ok = jnp.bool_(True)
        if dc == -1:
            ok = ok & (c > 0)
        if dc == 1:
            ok = ok & (c < chans - 1)
        if dt == -1:
            ok = ok & (t > 0)
        if dt == 1:
            ok = ok & (t < TM - 1)
        return ok

    arguments = [
        pltpu.make_async_copy(a, b, arg_sem.at[n])
        for n, (a, b) in enumerate(((rec_any, rec), (alive_any, alive), (taps_any, taps), (pat_any, pat)))
    ]
    for copy in arguments:
        copy.start()

    barrier = pltpu.get_barrier_semaphore()
    for d in range(1, TM):
        pl.semaphore_signal(barrier, inc=1, device_id=(c, lax.rem(t + d, TM)), device_id_type=MESH)
    for dc, dt in DIRS:
        if dc != 0:
            @pl.when(inside(dc, dt))
            def _():
                pl.semaphore_signal(barrier, inc=1, device_id=(c + dc, t + dt), device_id_type=MESH)

    slots[0] = jnp.zeros((48, 1024), jnp.bfloat16)
    slots[TM + 1] = jnp.zeros((48, 1024), jnp.bfloat16)
    for copy in arguments:
        copy.wait()

    eye = lax.broadcasted_iota(jnp.int32, (128, 128), 0) == lax.broadcasted_iota(jnp.int32, (128, 128), 1)
    row = jnp.broadcast_to(alive[...].astype(jnp.float32), (128, 128))
    lively = jnp.sum(jnp.where(eye, row, 0.0), axis=1, keepdims=True)
    rim[32:160, 256:1280] = rec[...] * lively
    pats[t, 0:8, :] = jnp.full((8, 128), pat[0, 0], jnp.int32)
    pats[t, 8:16, :] = jnp.full((8, 128), pat[0, 1], jnp.int32)

    @pl.when(c == 0)
    def _():
        rim[0:32, :] = jnp.zeros((32, 1536), jnp.float32)

    @pl.when(c == chans - 1)
    def _():
        rim[160:192, :] = jnp.zeros((32, 1536), jnp.float32)
        nbuf[128:176, :] = jnp.zeros((48, 1024), jnp.bfloat16)

    @pl.when(t == 0)
    def _():
        rim[:, 0:256] = jnp.zeros((192, 256), jnp.float32)

    @pl.when(t == TM - 1)
    def _():
        rim[:, 1280:1536] = jnp.zeros((192, 256), jnp.float32)

    peers = TM - 1 + jnp.where(c > 0, 1, 0) * (3 - jnp.where(t == 0, 1, 0) - jnp.where(t == TM - 1, 1, 0))
    peers = peers + jnp.where(c < chans - 1, 1, 0) * (3 - jnp.where(t == 0, 1, 0) - jnp.where(t == TM - 1, 1, 0))
    pl.semaphore_wait(barrier, peers)

    def halo(e, dc, dt, away=1):
        rs, rt, rn = ROWS[dc]
        cs, ct, cn = COLS[dt]
        return pltpu.make_async_remote_copy(
            src_ref=rim.at[pl.ds(rs, rn), pl.ds(cs, cn)],
            dst_ref=rim.at[pl.ds(rt, rn), pl.ds(ct, cn)],
            send_sem=halo_send.at[e], recv_sem=halo_recv.at[e],
            device_id=(c + away * dc, t + away * dt), device_id_type=MESH,
        )

    for e, (dc, dt) in enumerate(DIRS):
        @pl.when(inside(dc, dt))
        def _():
            halo(e, dc, dt).start()

    def pat_copy(d):
        return pltpu.make_async_remote_copy(
            src_ref=pats.at[t], dst_ref=pats.at[t], send_sem=pat_send.at[d], recv_sem=pat_recv.at[t],
            device_id=(c, lax.rem(t + d, TM)), device_id_type=MESH,
        )

    def send_pattern(d, _):
        pat_copy(d).start()
        return 0

    lax.fori_loop(1, TM, send_pattern, 0)

    acc[...] = jnp.zeros_like(acc)

    wide = jnp.concatenate([taps[...], jnp.zeros((1, 192), jnp.float32)], 1)
    band = pltpu.roll(jnp.broadcast_to(wide, (128, 256)), 0, 1, stride=1, stride_axis=0)[:, 0:192]
    inner = lax.broadcasted_iota(jnp.int32, (768, 256), 0)
    outer = lax.broadcasted_iota(jnp.int32, (768, 256), 1)
    boxcar = jnp.where((inner >= outer) & (inner <= outer + 512), 1.0, 0.0).astype(jnp.bfloat16)

    for e, (dc, dt) in enumerate(DIRS):
        @pl.when(inside(-dc, -dt))
        def _():
            halo(e, dc, dt, -1).wait_recv()

    def clean(b, _):
        cols = pl.ds(pl.multiple_of(256 * b, 256), 256)
        f = lively * jnp.dot(
            band, rim[:, cols], precision=lax.Precision.HIGHEST, preferred_element_type=jnp.float32
        )
        filtered[:, cols] = f
        rest = jnp.abs(f)
        for part in range(3):
            sizes[part, :, cols] = rest.astype(jnp.bfloat16)
            rest = rest - sizes[part, :, cols].astype(jnp.float32)
        return 0

    lax.fori_loop(0, 6, clean, 0)

    def scale(b, _):
        first = pl.multiple_of(256 * b, 256)
        total = None
        for part in range(3):
            s = jnp.dot(sizes[part, :, pl.ds(first, 768)], boxcar, preferred_element_type=jnp.float32)
            total = s if total is None else total + s
        level = total / (2 * HALF_WIN + 1)
        mine = filtered[:, pl.ds(first + 256, 256)]
        nbuf[0:128, pl.ds(first, 256)] = (mine / (level + 1e-5)).astype(jnp.bfloat16)
        return 0

    lax.fori_loop(0, 4, scale, 0)

    def up():
        return pltpu.make_async_remote_copy(
            src_ref=nbuf.at[pl.ds(0, 48), :], dst_ref=nbuf.at[pl.ds(128, 48), :],
            send_sem=up_send, recv_sem=up_recv, device_id=(c - 1, t), device_id_type=MESH,
        )

    @pl.when(c > 0)
    def _():
        up().start()

    def other(r):
        dx, dy = pick([d[0] for d in ORDER], r), pick([d[1] for d in ORDER], r)
        return lax.rem(t // 4 + dx, 2) * 4 + lax.rem(lax.rem(t, 4) + 4 - dy, 4)

    def source(r):
        dx, dy = pick([d[0] for d in ORDER], r), pick([d[1] for d in ORDER], r)
        return lax.rem(t // 4 + dx, 2) * 4 + lax.rem(lax.rem(t, 4) + dy, 4)

    def fill(dest, to):
        first = pl.multiple_of(dest * 16, 16)
        offsets = [jnp.concatenate([pats[dest, 8 * k : 8 * k + 8, :]] * 2, 0) for k in range(PAIRS)]
        for j in range(8):
            cols = slice(128 * j, 128 * j + 128)
            blocks = [nbuf[pl.ds(pl.multiple_of(first + 16 * o, 16), 16), cols] for o in range(4)]
            to[0:16, cols] = blocks[0]
            blocks = [block.astype(jnp.float32) for block in blocks]
            for k in range(PAIRS):
                chosen = blocks[0]
                for o in range(1, 4):
                    chosen = jnp.where(offsets[k] == o, blocks[o], chosen)
                to[16 * k + 16 : 16 * k + 32, cols] = chosen.astype(jnp.bfloat16)

    def deliver(r, dest):
        return pltpu.make_async_remote_copy(
            src_ref=pack.at[r], dst_ref=slots.at[t + 1], send_sem=send_sem.at[r], recv_sem=recv_sem.at[t],
            device_id=(c, dest), device_id_type=MESH,
        )

    def arrival(r):
        src = source(r)
        return pltpu.make_async_remote_copy(
            src_ref=pack.at[r], dst_ref=slots.at[src + 1], send_sem=send_sem.at[r], recv_sem=recv_sem.at[src],
            device_id=(c, src), device_id_type=MESH,
        )

    def await_pattern(d, _):
        src = lax.rem(t + d, TM)
        pltpu.make_async_remote_copy(
            src_ref=pats.at[src], dst_ref=pats.at[src], send_sem=pat_send.at[d], recv_sem=pat_recv.at[src],
            device_id=(c, src), device_id_type=MESH,
        ).wait_recv()
        return 0

    lax.fori_loop(1, TM, await_pattern, 0)

    def hand_out(n, _):
        r = lax.rem(n + 1, TM)
        dest = other(r)

        @pl.when((n == TM) & (c < chans - 1))
        def _():
            up().wait_recv()

        @pl.when((dest >= 5) == (n >= TM))
        def _():
            fill(dest, pack.at[r])

            @pl.when(r > 0)
            def _():
                deliver(r, dest).start()

            @pl.when(r == 0)
            def _():
                slots[t + 1] = pack[0]

        return 0

    lax.fori_loop(0, 2 * TM, hand_out, 0)

    steps, needs = schedule()

    def step(n, _):
        def take(r, _):
            arrival(r).wait_recv()
            return 0

        begin = jnp.where(n == 0, 0, look_up(needs, t, jnp.maximum(n - 1, 0)))
        lax.fori_loop(begin + 1, look_up(needs, t, n) + 1, take, 0)
        low = look_up(steps, t, n)
        accumulate(slots.at[low], slots.at[low + 1], acc, own, near, far, out, n == TM)
        return 0

    lax.fori_loop(0, TM + 1, step, 0)

    def finish(r, _):
        deliver(r, other(r)).wait_send()
        pat_copy(r).wait_send()
        return 0

    lax.fori_loop(1, TM, finish, 0)
    for e, (dc, dt) in enumerate(DIRS):
        @pl.when(inside(dc, dt))
        def _():
            halo(e, dc, dt).wait_send()

    @pl.when(c > 0)
    def _():
        up().wait_send()


def front(record, alive, taps, pattern):
    dma = pltpu.SemaphoreType.DMA
    return pl.pallas_call(
        front_kernel,
        out_shape=jax.ShapeDtypeStruct((PAIRS, BLOCK, BLOCK, 2 * LAG), jnp.float32),
        in_specs=[pl.BlockSpec(memory_space=pltpu.HBM)] * 4,
        out_specs=pl.BlockSpec(memory_space=pltpu.VMEM),
        scratch_shapes=[
            pltpu.VMEM((8, 256, 256), jnp.float32),
            pltpu.VMEM((128, 1024), jnp.float32),
            pltpu.VMEM((1, 128), jnp.int32),
            pltpu.VMEM((1, 64), jnp.float32),
            pltpu.SMEM((1, 2), jnp.int32),
            pltpu.VMEM((192, 1536), jnp.float32),
            pltpu.VMEM((176, 1024), jnp.bfloat16),
            pltpu.VMEM((TM, 48, 1024), jnp.bfloat16),
            pltpu.VMEM((TM, 16, 128), jnp.int32),
            pltpu.VMEM((TM + 2, 48, 1024), jnp.bfloat16),
            pltpu.VMEM((256, 1024), jnp.bfloat16),
            pltpu.VMEM((16, 1152), jnp.float32),
            pltpu.VMEM((256, 1920), jnp.bfloat16),
            pltpu.VMEM((128, 1536), jnp.float32),
            pltpu.VMEM((3, 128, 1536), jnp.bfloat16),
            dma((4,)), dma((8,)), dma((8,)), dma((TM,)), dma((TM,)), dma(()), dma(()), dma((TM,)), dma((TM,)),
        ],
        compiler_params=pltpu.CompilerParams(
            collective_id=0, has_side_effects=True, vmem_limit_bytes=32 << 20
        ),
        name="front",
    )(record, alive.reshape(1, 128), taps.reshape(1, 64), pattern)


def body(record, alive, taps, pattern):
    return front(record, alive, taps, pattern)[None]


def solution(mesh):
    placed = (P("chan", "tm"), P("chan"), P(), P(("chan", "tm"), None))
    return jax.shard_map(
        body,
        mesh=mesh,
        in_specs=placed,
        out_specs=P(("chan", "tm"), None, None, None, None),
        check_vma=False,
    )
```

time: 57.5 us -> 47 us (0.82)
  the two profiles are of different devices: /device:TPU:127 before, /device:TPU:219 now
where the time goes in v3:
time: 47 us; the launch traced here: 46.9 us
  Pallas kernels  42.5 us (90%)
  local copies, waits for them, and re-layouts  4.33 us (9%)
    pallas_call x1, Pallas kernels, front(): pl.pallas_call(front_kernel, out_shape=jax.ShapeDtypeStruct((PAIRS, BLOCK...  42.5 us
    unnamed x9, local copies, waits for them, and re-layouts  4.33 us

profile of v3, /device:TPU:219, one launch (start us, length us, event | category | flops | bytes accessed | tf_op | source)
XLA Modules:
  0.0 46.9 jit_solution(3253738230959322306)
XLA Ops:
  0.0 0.0 copy-start
  0.0 1.0 %copy-done = f32[128,1024]{1,0:T(8,128)S(1)} copy-done((f32[128,1024]{1,0:T(8,128)S(1)}, f32[128,1024]{1,0:T(8,128)}, u32[]{:S(2)}) %copy-start) | copy-done | bytes 524312
  1.0 0.0 copy-start.1
  1.0 0.7 %copy-done.1 = s32[128]{0:T(128)S(1)} copy-done((s32[128]{0:T(128)S(1)}, s32[128]{0:T(128)}, u32[]{:S(2)}) %copy-start.1) | copy-done | bytes 536
  1.7 0.0 copy-start.2
  1.7 0.7 %copy-done.2 = f32[64]{0:T(128)S(1)} copy-done((f32[64]{0:T(128)S(1)}, f32[64]{0:T(128)}, u32[]{:S(2)}) %copy-start.2) | copy-done | bytes 280
  2.4 0.0 copy-start.3
  2.4 0.7 %copy-done.3 = s32[1,2]{1,0:T(1,128)S(1)} copy-done((s32[1,2]{1,0:T(1,128)S(1)}, s32[1,2]{1,0:T(1,128)}, u32[]{:S(2)}) %copy-start.3) | copy-done | bytes 32
  3.0 42.5 %front.1 = f32[2,16,16,1024]{3,2,1,0:T(8,128)S(1)} custom-call(f32[128,1024]{1,0:T(8,128)S(1)} %copy-done, s32[1,128]{1,0:T(1,128)S(1)} %bitcast.4, f32[1,64]{1,0:T(1,128)S(1)} %bitcast.5, s32[1,2]{1,0:T(1,128)S(1)} %copy-done.3), custom_call_target="tpu_custom_call" | custom-call | tf_op jit(solution)/shard_map/front/pallas_call | solution.py:359
  45.5 1.3 %copy.6 = f32[1,2,16,16,1024]{4,3,2,1,0:T(8,128)} copy(f32[1,2,16,16,1024]{4,3,2,1,0:T(8,128)S(1)} %bitcast.3) | data formatting | bytes 4194304
Async XLA Ops:
  0.0 1.0 %copy-start = (f32[128,1024]{1,0:T(8,128)S(1)}, f32[128,1024]{1,0:T(8,128)}, u32[]{:S(2)}) copy-start(f32[128,1024]{1,0:T(8,128)} %rec_any.1) | copy-start | bytes 1572868
  1.0 0.7 %copy-start.1 = (s32[128]{0:T(128)S(1)}, s32[128]{0:T(128)}, u32[]{:S(2)}) copy-start(s32[128]{0:T(128)} %param.5) | copy-start | bytes 1540
  1.7 0.7 %copy-start.2 = (f32[64]{0:T(128)S(1)}, f32[64]{0:T(128)}, u32[]{:S(2)}) copy-start(f32[64]{0:T(128)} %param.6) | copy-start | bytes 772
  2.4 0.7 %copy-start.3 = (s32[1,2]{1,0:T(1,128)S(1)}, s32[1,2]{1,0:T(1,128)}, u32[]{:S(2)}) copy-start(s32[1,2]{1,0:T(1,128)} %pat_any.1) | copy-start | bytes 28

commit v4 on v3

--- a/solution.py
+++ b/solution.py
@@ -212,12 +212,16 @@
     outer = lax.broadcasted_iota(jnp.int32, (768, 256), 1)
     boxcar = jnp.where((inner >= outer) & (inner <= outer + 512), 1.0, 0.0).astype(jnp.bfloat16)
 
-    for e, (dc, dt) in enumerate(DIRS):
-        @pl.when(inside(-dc, -dt))
-        def _():
-            halo(e, dc, dt, -1).wait_recv()
-
-    def clean(b, _):
+    def await_halo(sides):
+        for e, (dc, dt) in enumerate(DIRS):
+            if (dt != 0) == sides:
+                @pl.when(inside(-dc, -dt))
+                def _():
+                    halo(e, dc, dt, -1).wait_recv()
+
+    await_halo(False)
+
+    def clean(b):
         cols = pl.ds(pl.multiple_of(256 * b, 256), 256)
         f = lively * jnp.dot(
             band, rim[:, cols], precision=lax.Precision.HIGHEST, preferred_element_type=jnp.float32
@@ -227,11 +231,8 @@
         for part in range(3):
             sizes[part, :, cols] = rest.astype(jnp.bfloat16)
             rest = rest - sizes[part, :, cols].astype(jnp.float32)
-        return 0
-
-    lax.fori_loop(0, 6, clean, 0)
-
-    def scale(b, _):
+
+    def scale(b):
         first = pl.multiple_of(256 * b, 256)
         total = None
         for part in range(3):
@@ -240,9 +241,28 @@
         level = total / (2 * HALF_WIN + 1)
         mine = filtered[:, pl.ds(first + 256, 256)]
         nbuf[0:128, pl.ds(first, 256)] = (mine / (level + 1e-5)).astype(jnp.bfloat16)
-        return 0
-
-    lax.fori_loop(0, 4, scale, 0)
+
+    turns = [(1, 1), (1, 2), (1, 3), (1, 4), (0, 1), (0, 2), (1, 0), (1, 5), (0, 0), (0, 3)]
+
+    def turn(n, _):
+        block = pick([b for _, b in turns], n)
+        cleans = pick([k for k, _ in turns], n)
+
+        @pl.when(n == 6)
+        def _():
+            await_halo(True)
+
+        @pl.when(cleans == 1)
+        def _():
+            clean(block)
+
+        @pl.when(cleans == 0)
+        def _():
+            scale(block)
+
+        return 0
+
+    lax.fori_loop(0, len(turns), turn, 0)
 
     def up():
         return pltpu.make_async_remote_copy(
@@ -300,14 +320,14 @@
     lax.fori_loop(1, TM, await_pattern, 0)
 
     def hand_out(n, _):
-        r = lax.rem(n + 1, TM)
+        r = pick([1, 2, 3, 1, 2, 3, 4, 5, 6, 7, 0], n)
         dest = other(r)
 
-        @pl.when((n == TM) & (c < chans - 1))
+        @pl.when((n == 3) & (c < chans - 1))
         def _():
             up().wait_recv()
 
-        @pl.when((dest >= 5) == (n >= TM))
+        @pl.when((n >= 6) | ((dest >= 5) == (n >= 3)))
         def _():
             fill(dest, pack.at[r])
 
@@ -321,7 +341,11 @@
 
         return 0
 
-    lax.fori_loop(0, 2 * TM, hand_out, 0)
+    lax.fori_loop(0, 11, hand_out, 0)
+
+    def follow(done, r):
+        deliver(done, other(done)).wait_send()
+        deliver(r, other(r)).start()
 
     steps, needs = schedule()
 
@@ -340,6 +364,7 @@
 
     def finish(r, _):
         deliver(r, other(r)).wait_send()
+
         pat_copy(r).wait_send()
         return 0
 

time: 47 us -> 46.1 us (0.981)
  the two profiles are of different devices: /device:TPU:219 before, /device:TPU:127 now
where the time goes in v4:
time: 46.1 us; the launch traced here: 45.5 us
  Pallas kernels  41.2 us (89%)
  local copies, waits for them, and re-layouts  4.33 us (9%)
    pallas_call x1, Pallas kernels, front(): pl.pallas_call(front_kernel, out_shape=jax.ShapeDtypeStruct((PAIRS, BLOCK...  41.2 us
    unnamed x9, local copies, waits for them, and re-layouts  4.33 us

profile of v4, /device:TPU:127, one launch (start us, length us, event | category | flops | bytes accessed | tf_op | source)
XLA Modules:
  0.0 45.5 jit_solution(10159529862755829432)
XLA Ops:
  0.0 0.0 copy-start
  0.0 1.0 %copy-done = f32[128,1024]{1,0:T(8,128)S(1)} copy-done((f32[128,1024]{1,0:T(8,128)S(1)}, f32[128,1024]{1,0:T(8,128)}, u32[]{:S(2)}) %copy-start) | copy-done | bytes 524312
  1.0 0.0 copy-start.1
  1.0 0.7 %copy-done.1 = s32[128]{0:T(128)S(1)} copy-done((s32[128]{0:T(128)S(1)}, s32[128]{0:T(128)}, u32[]{:S(2)}) %copy-start.1) | copy-done | bytes 536
  1.7 0.0 copy-start.2
  1.7 0.7 %copy-done.2 = f32[64]{0:T(128)S(1)} copy-done((f32[64]{0:T(128)S(1)}, f32[64]{0:T(128)}, u32[]{:S(2)}) %copy-start.2) | copy-done | bytes 280
  2.4 0.0 copy-start.3
  2.4 0.7 %copy-done.3 = s32[1,2]{1,0:T(1,128)S(1)} copy-done((s32[1,2]{1,0:T(1,128)S(1)}, s32[1,2]{1,0:T(1,128)}, u32[]{:S(2)}) %copy-start.3) | copy-done | bytes 32
  3.0 41.2 %front.1 = f32[2,16,16,1024]{3,2,1,0:T(8,128)S(1)} custom-call(f32[128,1024]{1,0:T(8,128)S(1)} %copy-done, s32[1,128]{1,0:T(1,128)S(1)} %bitcast.4, f32[1,64]{1,0:T(1,128)S(1)} %bitcast.5, s32[1,2]{1,0:T(1,128)S(1)} %copy-done.3), custom_call_target="tpu_custom_call" | custom-call | tf_op jit(solution)/shard_map/front/pallas_call | solution.py:384
  44.2 1.3 %copy.6 = f32[1,2,16,16,1024]{4,3,2,1,0:T(8,128)} copy(f32[1,2,16,16,1024]{4,3,2,1,0:T(8,128)S(1)} %bitcast.3) | data formatting | bytes 4194304
Async XLA Ops:
  0.0 1.0 %copy-start = (f32[128,1024]{1,0:T(8,128)S(1)}, f32[128,1024]{1,0:T(8,128)}, u32[]{:S(2)}) copy-start(f32[128,1024]{1,0:T(8,128)} %rec_any.1) | copy-start | bytes 1572868
  1.0 0.7 %copy-start.1 = (s32[128]{0:T(128)S(1)}, s32[128]{0:T(128)}, u32[]{:S(2)}) copy-start(s32[128]{0:T(128)} %param.5) | copy-start | bytes 1540
  1.7 0.7 %copy-start.2 = (f32[64]{0:T(128)S(1)}, f32[64]{0:T(128)}, u32[]{:S(2)}) copy-start(f32[64]{0:T(128)} %param.6) | copy-start | bytes 772
  2.4 0.7 %copy-start.3 = (s32[1,2]{1,0:T(1,128)S(1)}, s32[1,2]{1,0:T(1,128)}, u32[]{:S(2)}) copy-start(s32[1,2]{1,0:T(1,128)} %pat_any.1) | copy-start | bytes 28

commit v5 on v4

--- a/solution.py
+++ b/solution.py
@@ -54,7 +54,7 @@
 COLS = {-1: (256, 1280, 256), 0: (256, 256, 1024), 1: (1024, 0, 256)}
 
 
-def accumulate(low, high, acc, own, near, far, out, last):
+def accumulate(low, high, acc, own, near, far):
     lane = lax.broadcasted_iota(jnp.int32, (8, 128), 1)
     sub = lax.broadcasted_iota(jnp.int32, (8, 128), 0)
     near[:, 0:640] = low[0:16, 384:1024].astype(jnp.float32)
@@ -83,10 +83,6 @@
     for qh in range(8):
         acc[qh] += product(qh)
 
-    @pl.when(last)
-    def _():
-        lax.fori_loop(0, 8, functools.partial(transpose, acc, out), 0)
-
 
 def transpose(acc, out, qh, _):
     group = lax.broadcasted_iota(jnp.int32, (8, 128), 1) // 16
@@ -96,7 +92,7 @@
                 first = 16 * k + 8 * jh
                 xs = []
                 for ql in range(8):
-                    x = acc[qh, 32 * ql + first : 32 * ql + first + 8, 128 * ih : 128 * ih + 128] * (1.0 / math.sqrt(T))
+                    x = acc[qh, 32 * ql + first : 32 * ql + first + 8, 128 * ih : 128 * ih + 128]
                     xs.append(pltpu.roll(x, 16 * ql, 1) if ql else x)
                 xs = [xs[-m % 8] for m in range(8)]
                 for bit in (1, 2, 4):
@@ -109,8 +105,8 @@
 
 
 def front_kernel(
-    rec_any, alive_any, taps_any, pat_any, out, acc, rec, alive, taps, pat, rim, nbuf, pack, pats, slots, own, near, far, filtered, sizes,
-    arg_sem, halo_send, halo_recv, pat_send, pat_recv, up_send, up_recv, send_sem, recv_sem,
+    rec_any, alive_any, taps_any, pat_any, final, acc, out, rec, alive, taps, pat, rim, nbuf, pack, pats, slots, own, near, far, filtered, sizes,
+    out_sem, arg_sem, halo_send, halo_recv, pat_send, pat_recv, up_send, up_recv, send_sem, recv_sem,
 ):
     c = lax.axis_index("chan")
     t = lax.axis_index("tm")
@@ -242,6 +238,18 @@
         mine = filtered[:, pl.ds(first + 256, 256)]
         nbuf[0:128, pl.ds(first, 256)] = (mine / (level + 1e-5)).astype(jnp.bfloat16)
 
+    def up(piece):
+        cols = pl.ds(*((256, 512), (0, 256), (768, 256))[piece])
+        return pltpu.make_async_remote_copy(
+            src_ref=nbuf.at[pl.ds(0, 48), cols], dst_ref=nbuf.at[pl.ds(128, 48), cols],
+            send_sem=up_send.at[piece], recv_sem=up_recv.at[piece], device_id=(c - 1, t), device_id_type=MESH,
+        )
+
+    def up_start(piece):
+        @pl.when(c > 0)
+        def _():
+            up(piece).start()
+
     turns = [(1, 1), (1, 2), (1, 3), (1, 4), (0, 1), (0, 2), (1, 0), (1, 5), (0, 0), (0, 3)]
 
     def turn(n, _):
@@ -250,6 +258,7 @@
 
         @pl.when(n == 6)
         def _():
+            up_start(0)
             await_halo(True)
 
         @pl.when(cleans == 1)
@@ -264,15 +273,8 @@
 
     lax.fori_loop(0, len(turns), turn, 0)
 
-    def up():
-        return pltpu.make_async_remote_copy(
-            src_ref=nbuf.at[pl.ds(0, 48), :], dst_ref=nbuf.at[pl.ds(128, 48), :],
-            send_sem=up_send, recv_sem=up_recv, device_id=(c - 1, t), device_id_type=MESH,
-        )
-
-    @pl.when(c > 0)
-    def _():
-        up().start()
+    up_start(1)
+    up_start(2)
 
     def other(r):
         dx, dy = pick([d[0] for d in ORDER], r), pick([d[1] for d in ORDER], r)
@@ -325,7 +327,8 @@
 
         @pl.when((n == 3) & (c < chans - 1))
         def _():
-            up().wait_recv()
+            for piece in range(3):
+                up(piece).wait_recv()
 
         @pl.when((n >= 6) | ((dest >= 5) == (n >= 3)))
         def _():
@@ -357,10 +360,25 @@
         begin = jnp.where(n == 0, 0, look_up(needs, t, jnp.maximum(n - 1, 0)))
         lax.fori_loop(begin + 1, look_up(needs, t, n) + 1, take, 0)
         low = look_up(steps, t, n)
-        accumulate(slots.at[low], slots.at[low + 1], acc, own, near, far, out, n == TM)
+        accumulate(slots.at[low], slots.at[low + 1], acc, own, near, far)
         return 0
 
     lax.fori_loop(0, TM + 1, step, 0)
+
+    def put(qh):
+        cols = pl.ds(pl.multiple_of(128 * qh, 128), 128)
+        return pltpu.make_async_copy(out.at[:, :, :, cols], final.at[:, :, :, cols], out_sem.at[qh])
+
+    def turn_over(qh, _):
+        transpose(acc, out, qh, 0)
+        put(qh).start()
+        return 0
+
+    def written(qh, _):
+        put(qh).wait()
+        return 0
+
+    lax.fori_loop(0, 8, turn_over, 0)
 
     def finish(r, _):
         deliver(r, other(r)).wait_send()
@@ -376,7 +394,10 @@
 
     @pl.when(c > 0)
     def _():
-        up().wait_send()
+        for piece in range(3):
+            up(piece).wait_send()
+
+    lax.fori_loop(0, 8, written, 0)
 
 
 def front(record, alive, taps, pattern):
@@ -385,9 +406,10 @@
         front_kernel,
         out_shape=jax.ShapeDtypeStruct((PAIRS, BLOCK, BLOCK, 2 * LAG), jnp.float32),
         in_specs=[pl.BlockSpec(memory_space=pltpu.HBM)] * 4,
-        out_specs=pl.BlockSpec(memory_space=pltpu.VMEM),
+        out_specs=pl.BlockSpec(memory_space=pl.ANY),
         scratch_shapes=[
             pltpu.VMEM((8, 256, 256), jnp.float32),
+            pltpu.VMEM((PAIRS, BLOCK, BLOCK, 2 * LAG), jnp.float32),
             pltpu.VMEM((128, 1024), jnp.float32),
             pltpu.VMEM((1, 128), jnp.int32),
             pltpu.VMEM((1, 64), jnp.float32),
@@ -402,17 +424,17 @@
             pltpu.VMEM((256, 1920), jnp.bfloat16),
             pltpu.VMEM((128, 1536), jnp.float32),
             pltpu.VMEM((3, 128, 1536), jnp.bfloat16),
-            dma((4,)), dma((8,)), dma((8,)), dma((TM,)), dma((TM,)), dma(()), dma(()), dma((TM,)), dma((TM,)),
+            dma((8,)), dma((4,)), dma((8,)), dma((8,)), dma((TM,)), dma((TM,)), dma((3,)), dma((3,)), dma((TM,)), dma((TM,)),
         ],
         compiler_params=pltpu.CompilerParams(
-            collective_id=0, has_side_effects=True, vmem_limit_bytes=32 << 20
+            collective_id=0, has_side_effects=True, vmem_limit_bytes=60 << 20
         ),
         name="front",
     )(record, alive.reshape(1, 128), taps.reshape(1, 64), pattern)
 
 
 def body(record, alive, taps, pattern):
-    return front(record, alive, taps, pattern)[None]
+    return front(record, alive, taps, pattern)[None] * (1.0 / math.sqrt(T))
 
 
 def solution(mesh):

time: 46.1 us -> 45.2 us (0.980)
  local copies, waits for them, and re-layouts: 4.33 us -> 0 us
  other arithmetic: 0 us -> 3.29 us
  Pallas kernels: 41.2 us -> 41.8 us
    unnamed x9 -> x0, local copies, waits for them, and re-layouts: 4.33 us -> none
    mul x0 -> x1, other arithmetic: none -> 3.29 us  [body(): return front(record, alive, taps, pattern)[None] * (1.0 / math.sqrt(T))]
    pallas_call x1, Pallas kernels: 41.2 us -> 41.8 us  [front(): pl.pallas_call(front_kernel, out_shape=jax.ShapeDtypeStruct((PAIRS, BLOCK...]
where the time goes in v5:
time: 45.2 us; the launch traced here: 45.1 us
  Pallas kernels  41.8 us (92%)
  other arithmetic  3.29 us (7%)
    pallas_call x1, Pallas kernels, front(): pl.pallas_call(front_kernel, out_shape=jax.ShapeDtypeStruct((PAIRS, BLOCK...  41.8 us
    mul x1, other arithmetic, body(): return front(record, alive, taps, pattern)[None] * (1.0 / math.sqrt(T))  3.29 us

profile of v5, /device:TPU:127, one launch (start us, length us, event | category | flops | bytes accessed | tf_op | source)
XLA Modules:
  0.0 45.1 jit_solution(3753360424384002713)
XLA Ops:
  0.0 41.8 %front.1 = f32[2,16,16,1024]{3,2,1,0:T(8,128)} custom-call(f32[128,1024]{1,0:T(8,128)} %rec_any.1, s32[1,128]{1,0:T(1,128)} %bitcast.4, f32[1,64]{1,0:T(1,128)} %bitcast.5, s32[1,2]{1,0:T(1,128)} %pat_any.1), custom_call_target="tpu_custom_call" | custom-call | tf_op jit(solution)/shard_map/front/pallas_call | solution.py:405
  41.8 3.3 %multiply_bitcast_fusion = f32[1,2,16,16,1024]{4,3,2,1,0:T(8,128)} fusion(f32[2,16,16,1024]{3,2,1,0:T(8,128)} %front.1), kind=kLoop, calls=%fused_computation | loop fusion | flops 524288 | bytes 4194304 | tf_op jit(solution)/shard_map/mul | solution.py:437

commit v6 on v5

--- a/solution.py
+++ b/solution.py
@@ -322,15 +322,15 @@
     lax.fori_loop(1, TM, await_pattern, 0)
 
     def hand_out(n, _):
-        r = pick([1, 2, 3, 1, 2, 3, 4, 5, 6, 7, 0], n)
+        r = lax.rem(n + 1, TM)
         dest = other(r)
 
-        @pl.when((n == 3) & (c < chans - 1))
+        @pl.when((n == TM) & (c < chans - 1))
         def _():
             for piece in range(3):
                 up(piece).wait_recv()
 
-        @pl.when((n >= 6) | ((dest >= 5) == (n >= 3)))
+        @pl.when((dest >= 5) == (n >= TM))
         def _():
             fill(dest, pack.at[r])
 
@@ -344,7 +344,7 @@
 
         return 0
 
-    lax.fori_loop(0, 11, hand_out, 0)
+    lax.fori_loop(0, 2 * TM, hand_out, 0)
 
     def follow(done, r):
         deliver(done, other(done)).wait_send()

time: 45.2 us -> 45.6 us (level)
  no operation moved by 1% of the time
where the time goes in v6:
time: 45.6 us; the launch traced here: 45.4 us
  Pallas kernels  42.1 us (92%)
  other arithmetic  3.29 us (7%)
    pallas_call x1, Pallas kernels, front(): pl.pallas_call(front_kernel, out_shape=jax.ShapeDtypeStruct((PAIRS, BLOCK...  42.1 us
    mul x1, other arithmetic, body(): return front(record, alive, taps, pattern)[None] * (1.0 / math.sqrt(T))  3.29 us

profile of v6, /device:TPU:127, one launch (start us, length us, event | category | flops | bytes accessed | tf_op | source)
XLA Modules:
  0.0 45.4 jit_solution(13081996277278968937)
XLA Ops:
  0.0 42.1 %front.1 = f32[2,16,16,1024]{3,2,1,0:T(8,128)} custom-call(f32[128,1024]{1,0:T(8,128)} %rec_any.1, s32[1,128]{1,0:T(1,128)} %bitcast.4, f32[1,64]{1,0:T(1,128)} %bitcast.5, s32[1,2]{1,0:T(1,128)} %pat_any.1), custom_call_target="tpu_custom_call" | custom-call | tf_op jit(solution)/shard_map/front/pallas_call | solution.py:405
  42.2 3.3 %multiply_bitcast_fusion = f32[1,2,16,16,1024]{4,3,2,1,0:T(8,128)} fusion(f32[2,16,16,1024]{3,2,1,0:T(8,128)} %front.1), kind=kLoop, calls=%fused_computation | loop fusion | flops 524288 | bytes 4194304 | tf_op jit(solution)/shard_map/mul | solution.py:437
